TPU v7x, 32 devices: a whole 2x2x4 slice. The times are simulated.
32 devices in a mesh: section: 2 (over core), batch: 16 (over z, y, x).
Axes of the slice: x: 2, y: 2, z: 4, core: 2. Of those that a mesh axis runs over, the one named last changes fastest.
Arguments:
- enc_input: bfloat16 [64, 228, 768], P('batch'), may hold values from -6 to 6
- dec_input: bfloat16 [64, 32, 768], P('batch'), may hold values from -6 to 6
- out_grad: bfloat16 [64, 32, 768], P('batch'), may hold values from -6 to 6
- attn_qkv: bfloat16 [2, 768, 2304], P('section'), may hold values from -0.21875 to 0.21875
- attn_out: bfloat16 [2, 768, 768], P('section'), may hold values from -0.875 to 0.875
- mlp_in: bfloat16 [2, 768, 3072], P('section'), may hold values from -0.21875 to 0.21875
- mlp_out: bfloat16 [2, 3072, 768], P('section'), may hold values from -0.109375 to 0.109375
- cross_proj: bfloat16 [2, 768, 1536], P('section'), may hold values from -0.3125 to 0.3125
- norm_gain: bfloat16 [2, 3, 768], P('section'), may hold values from 0.099609375 to 1.8984375
- norm_shift: bfloat16 [2, 3, 768], P('section'), may hold values from -2 to 2
- image_count: int32 [16], P('batch'), may hold values from 0 to 4
- prefix_len: int32 [64], P('batch'), may hold values from 1 to 32
- suffix_len: int32 [64], P('batch'), may hold values from 1 to 32
Outputs:
- decoded: bfloat16 [64, 32, 768], P('batch', None, 'section')
- enc_input_grad: bfloat16 [64, 228, 768], P('batch', None, 'section')
- dec_input_grad: bfloat16 [64, 32, 768], P('batch', None, 'section')
- grad_attn_qkv: float32 [2, 768, 2304], P('section')
- grad_attn_out: float32 [2, 768, 768], P('section')
- grad_mlp_in: float32 [2, 768, 3072], P('section')
- grad_mlp_out: float32 [2, 3072, 768], P('section')
- grad_cross_proj: float32 [2, 768, 1536], P('section')
- grad_norm_gain: float32 [2, 3, 768], P('section')
- grad_norm_shift: float32 [2, 3, 768], P('section')
Inputs may be any that keep to these rules, and one draw needn't show every extreme that they name: `image_count`: the items of a batch shard whose local number is below this count carry image patches; the patch positions of the others are masked. `prefix_len`: prefix positions at or beyond this length are padding. `suffix_len`: suffix positions at or beyond this length are padding as keys.
All inputs are finite; a program needn't handle non-finite values.
Results may differ from a plain program's by a relative error of at most 0.019.
Values may be sent and summed in bfloat16 or wider, within the bound.
A program may use at most 512 MiB of HBM per device.

v0:
```python
import jax
import jax.numpy as jnp
from jax import lax
from jax.sharding import PartitionSpec as P

HEAD_DIM = 64
PATCHES = 196
MICRO = 4


far_below = -1000000000.0
epsilon = 1e-06


def from_behind(shard, axis, by):
    size = lax.axis_size(axis)
    pairs = [(i, i + by) for i in range(size) if 0 <= i + by < size]
    return lax.ppermute(shard, axis, pairs)


def shortened(shard):
    return jax.tree.map(lambda a: a.astype(jnp.bfloat16) if a.dtype == jnp.float32 else a, shard)


def swapped_2(shard, axis, stride):
    return lax.ppermute(shard, axis, [(i, i ^ 1 << stride) for i in range(lax.axis_size(axis))])


def layer_norm(inputs, gain_row, shift_row):
    average = jnp.mean(inputs, axis=-1, keepdims=True)
    centered = inputs - average
    variance = jnp.mean(centered * centered, axis=-1, keepdims=True)
    return centered * lax.rsqrt(variance + epsilon) * gain_row + shift_row


def norm_back(inputs, gain_row, shift_row, grad_normed):
    unused, pullback = jax.vjp(layer_norm, inputs, gain_row, shift_row)
    return pullback(grad_normed)


def gelu_back(upward, grad_active):
    unused, pullback = jax.vjp(jax.nn.gelu, upward)
    return pullback(grad_active)[0]


def forward_product(left_side, matrix):
    return jnp.einsum("bld,df->blf", left_side, matrix, preferred_element_type=jnp.float32)


def backward_product(grad_rows, matrix):
    return jnp.einsum("blf,df->bld", grad_rows, matrix, preferred_element_type=jnp.float32)


def weight_product(left_side, grad_rows):
    return jnp.einsum("bld,blf->df", left_side, grad_rows, preferred_element_type=jnp.float32)


def split_heads(rows):
    return rows.reshape(rows.shape[0], rows.shape[1], -1, HEAD_DIM)


def masked_scores(query_heads, key_heads, allowed):
    scores = jnp.einsum(
        "bqhe,bkhe->bhqk", query_heads, key_heads, preferred_element_type=jnp.float32
    ) * HEAD_DIM ** (-0.5)
    return jnp.where(allowed[:, None], scores, far_below)


def attend(queries, key_rows, value_rows, allowed):
    scores = masked_scores(split_heads(queries), split_heads(key_rows), allowed)
    row_top = jnp.max(scores, axis=-1, keepdims=True)
    log_total = row_top + jnp.log(jnp.sum(jnp.exp(scores - row_top), axis=-1, keepdims=True))
    probability = jnp.exp(scores - log_total).astype(jnp.bfloat16)
    attended = jnp.einsum(
        "bhqk,bkhe->bqhe", probability, split_heads(value_rows), preferred_element_type=jnp.float32
    )
    return (attended.reshape(queries.shape).astype(jnp.bfloat16), log_total)


def attend_back(queries, key_rows, value_rows, allowed, log_total, grad_attended):
    query_heads = split_heads(queries)
    key_heads = split_heads(key_rows)
    value_heads = split_heads(value_rows)
    probability = jnp.exp(masked_scores(query_heads, key_heads, allowed) - log_total)
    grad_heads = split_heads(grad_attended)
    grad_probability = jnp.einsum(
        "bqhe,bkhe->bhqk", grad_heads, value_heads, preferred_element_type=jnp.float32
    )
    grad_values = jnp.einsum(
        "bhqk,bqhe->bkhe",
        probability.astype(jnp.bfloat16),
        grad_heads,
        preferred_element_type=jnp.float32,
    )
    inner = jnp.sum(probability * grad_probability, axis=-1, keepdims=True)
    grad_scores = (probability * (grad_probability - inner)).astype(jnp.bfloat16)
    grad_queries = jnp.einsum(
        "bhqk,bkhe->bqhe", grad_scores, key_heads, preferred_element_type=jnp.float32
    ) * HEAD_DIM ** (-0.5)
    grad_keys = jnp.einsum(
        "bhqk,bqhe->bkhe", grad_scores, query_heads, preferred_element_type=jnp.float32
    ) * HEAD_DIM ** (-0.5)
    return (
        grad_queries.reshape(queries.shape),
        grad_keys.reshape(key_rows.shape),
        grad_values.reshape(value_rows.shape),
    )


def self_attention(inputs, gain_row, shift_row, qkv_matrix, out_matrix, allowed):
    normed = layer_norm(inputs, gain_row, shift_row).astype(jnp.bfloat16)
    qkv = forward_product(normed, qkv_matrix).astype(jnp.bfloat16)
    queries, key_rows, value_rows = jnp.split(qkv, 3, axis=-1)
    attended, log_total = attend(queries, key_rows, value_rows, allowed)
    return ((normed, qkv, attended, log_total), forward_product(attended, out_matrix))


def self_attention_back(
    inputs, gain_row, shift_row, qkv_matrix, out_matrix, allowed, kept, grad_stream
):
    normed, qkv, attended, log_total = kept
    grad_low = grad_stream.astype(jnp.bfloat16)
    grad_out_matrix = weight_product(attended, grad_low)
    grad_attended = backward_product(grad_low, out_matrix).astype(jnp.bfloat16)
    queries, key_rows, value_rows = jnp.split(qkv, 3, axis=-1)
    grad_parts = attend_back(queries, key_rows, value_rows, allowed, log_total, grad_attended)
    grad_qkv = jnp.concatenate(grad_parts, axis=-1).astype(jnp.bfloat16)
    grad_qkv_matrix = weight_product(normed, grad_qkv)
    grad_inputs, grad_gain, grad_shift = norm_back(
        inputs, gain_row, shift_row, backward_product(grad_qkv, qkv_matrix)
    )
    return (grad_stream + grad_inputs, grad_qkv_matrix, grad_out_matrix, grad_gain, grad_shift)


def feed_forward(hidden, gain_row, shift_row, up_matrix, down_matrix):
    normed = layer_norm(hidden, gain_row, shift_row).astype(jnp.bfloat16)
    upward = forward_product(normed, up_matrix)
    active = jax.nn.gelu(upward).astype(jnp.bfloat16)
    return (normed, upward, active, forward_product(active, down_matrix))


def feed_forward_back(hidden, gain_row, shift_row, up_matrix, down_matrix, kept, grad_stream):
    normed, upward, active, unused = kept
    grad_low = grad_stream.astype(jnp.bfloat16)
    grad_down = weight_product(active, grad_low)
    grad_upward = gelu_back(upward, backward_product(grad_low, down_matrix)).astype(jnp.bfloat16)
    grad_up = weight_product(normed, grad_upward)
    grad_hidden, grad_gain, grad_shift = norm_back(
        hidden, gain_row, shift_row, backward_product(grad_upward, up_matrix)
    )
    return (grad_stream + grad_hidden, grad_up, grad_down, grad_gain, grad_shift)


def encoder_pass(enc_block, allowed, weights):
    qkv_matrix, out_matrix, up_matrix, down_matrix, cross_matrix, gains, shifts = weights
    inputs = enc_block.astype(jnp.float32)
    kept_attention, branch = self_attention(
        inputs, gains[0], shifts[0], qkv_matrix, out_matrix, allowed
    )
    hidden = inputs + branch
    kept_forward = feed_forward(hidden, gains[1], shifts[1], up_matrix, down_matrix)
    result = hidden + kept_forward[3]
    memory = layer_norm(result, gains[2], shifts[2]).astype(jnp.bfloat16)
    keys_values = forward_product(memory, cross_matrix).astype(jnp.bfloat16)
    return ((inputs, kept_attention, hidden, kept_forward, result, memory), keys_values)


def zero_encoder_kept(items, enc_len, model_width, hidden_units):
    heads = model_width // HEAD_DIM
    wide_float = jnp.zeros((items, enc_len, model_width), jnp.float32)
    wide_low = jnp.zeros((items, enc_len, model_width), jnp.bfloat16)
    kept_attention = (
        wide_low,
        jnp.zeros((items, enc_len, 3 * model_width), jnp.bfloat16),
        wide_low,
        jnp.zeros((items, heads, enc_len, 1), jnp.float32),
    )
    kept_forward = (
        wide_low,
        jnp.zeros((items, enc_len, hidden_units), jnp.float32),
        jnp.zeros((items, enc_len, hidden_units), jnp.bfloat16),
        wide_float,
    )
    return (wide_float, kept_attention, wide_float, kept_forward, wide_float, wide_low)


def encoder_back(kept, allowed, weights, grad_keys_values):
    qkv_matrix, out_matrix, up_matrix, down_matrix, cross_matrix, gains, shifts = weights
    inputs, kept_attention, hidden, kept_forward, result, memory = kept
    grad_cross = weight_product(memory, grad_keys_values)
    grad_result, gain_two, shift_two = norm_back(
        result, gains[2], shifts[2], backward_product(grad_keys_values, cross_matrix)
    )
    grad_hidden, grad_up, grad_down, gain_one, shift_one = feed_forward_back(
        hidden, gains[1], shifts[1], up_matrix, down_matrix, kept_forward, grad_result
    )
    grad_inputs, grad_qkv, grad_attn_out, gain_zero, shift_zero = self_attention_back(
        inputs, gains[0], shifts[0], qkv_matrix, out_matrix, allowed, kept_attention, grad_hidden
    )
    grads = (
        grad_qkv,
        grad_attn_out,
        grad_up,
        grad_down,
        grad_cross,
        jnp.stack([gain_zero, gain_one, gain_two]),
        jnp.stack([shift_zero, shift_one, shift_two]),
    )
    return (grad_inputs.astype(jnp.bfloat16), grads)


def decoder_pass(dec_block, grad_block, keys_values, self_allowed, cross_allowed, weights):
    qkv_matrix, out_matrix, up_matrix, down_matrix, cross_matrix, gains, shifts = weights
    model_width = cross_matrix.shape[0]
    query_matrix = cross_matrix[:, :model_width]
    back_matrix = cross_matrix[:, model_width:]
    inputs = dec_block.astype(jnp.float32)
    kept_attention, branch = self_attention(
        inputs, gains[0], shifts[0], qkv_matrix, out_matrix, self_allowed
    )
    hidden = inputs + branch
    cross_normed = layer_norm(hidden, gains[1], shifts[1]).astype(jnp.bfloat16)
    cross_queries = forward_product(cross_normed, query_matrix).astype(jnp.bfloat16)
    key_rows, value_rows = jnp.split(keys_values, 2, axis=-1)
    cross_attended, cross_log = attend(cross_queries, key_rows, value_rows, cross_allowed)
    middle = hidden + forward_product(cross_attended, back_matrix)
    kept_forward = feed_forward(middle, gains[2], shifts[2], up_matrix, down_matrix)
    result = middle + kept_forward[3]
    grad_result = grad_block.astype(jnp.float32)
    grad_middle, grad_up, grad_down, gain_two, shift_two = feed_forward_back(
        middle, gains[2], shifts[2], up_matrix, down_matrix, kept_forward, grad_result
    )
    grad_low = grad_middle.astype(jnp.bfloat16)
    grad_back_matrix = weight_product(cross_attended, grad_low)
    grad_cross_attended = backward_product(grad_low, back_matrix).astype(jnp.bfloat16)
    grad_cross_queries, grad_key_rows, grad_value_rows = attend_back(
        cross_queries, key_rows, value_rows, cross_allowed, cross_log, grad_cross_attended
    )
    grad_keys_values = jnp.concatenate([grad_key_rows, grad_value_rows], axis=-1).astype(
        jnp.bfloat16
    )
    grad_queries_low = grad_cross_queries.astype(jnp.bfloat16)
    grad_query_matrix = weight_product(cross_normed, grad_queries_low)
    grad_norm_input, gain_one, shift_one = norm_back(
        hidden, gains[1], shifts[1], backward_product(grad_queries_low, query_matrix)
    )
    grad_hidden = grad_middle + grad_norm_input
    grad_inputs, grad_qkv, grad_attn_out, gain_zero, shift_zero = self_attention_back(
        inputs,
        gains[0],
        shifts[0],
        qkv_matrix,
        out_matrix,
        self_allowed,
        kept_attention,
        grad_hidden,
    )
    grads = (
        grad_qkv,
        grad_attn_out,
        grad_up,
        grad_down,
        jnp.concatenate([grad_query_matrix, grad_back_matrix], axis=1),
        jnp.stack([gain_zero, gain_one, gain_two]),
        jnp.stack([shift_zero, shift_one, shift_two]),
    )
    return (result.astype(jnp.bfloat16), grad_inputs.astype(jnp.bfloat16), grad_keys_values, grads)


def encoder_keys(has_image, prefix_rows, enc_len):
    positions = jnp.arange(enc_len, dtype=jnp.int32)
    patch_part = positions[None, :] < PATCHES
    return jnp.where(
        patch_part, has_image[:, None], positions[None, :] - PATCHES < prefix_rows[:, None]
    )[:, None, :]


def decoder_mask(suffix_rows, dec_len):
    positions = jnp.arange(dec_len, dtype=jnp.int32)
    return (positions[None, None, :] <= positions[None, :, None]) & (
        positions[None, None, :] < suffix_rows[:, None, None]
    )


def per_device(
    enc_input,
    dec_input,
    out_grad,
    attn_qkv,
    attn_out,
    mlp_in,
    mlp_out,
    cross_proj,
    norm_gain,
    norm_shift,
    image_count,
    prefix_len,
    suffix_len,
):
    section_index = lax.axis_index("section")
    items_dev = enc_input.shape[0]
    per_step = items_dev // MICRO
    enc_len = enc_input.shape[1]
    dec_len = dec_input.shape[1]
    model_width = enc_input.shape[2]
    hidden_units = mlp_in.shape[2]
    weights = (
        attn_qkv[0],
        attn_out[0],
        mlp_in[0],
        mlp_out[0],
        cross_proj[0],
        norm_gain[0].astype(jnp.float32),
        norm_shift[0].astype(jnp.float32),
    )
    has_image = jnp.arange(items_dev, dtype=jnp.int32) < image_count[0]
    key_allowed = encoder_keys(has_image, prefix_len, enc_len)
    self_allowed = decoder_mask(suffix_len, dec_len)
    zero_send = jnp.zeros((per_step, enc_len, 2 * model_width), jnp.bfloat16)
    zero_enc = jnp.zeros((per_step, enc_len, model_width), jnp.bfloat16)
    zero_dec = jnp.zeros((per_step, dec_len, model_width), jnp.bfloat16)
    zero_grads = tuple((jnp.zeros(matrix.shape, jnp.float32) for matrix in weights))
    zero_kept = zero_encoder_kept(per_step, enc_len, model_width, hidden_units)

    def rows_of(array, step_index):
        return array[step_index * per_step : (step_index + 1) * per_step]

    arrived = zero_send
    returned = zero_send
    stored = []
    enc_grad_blocks = []
    dec_out_blocks = []
    dec_grad_blocks = []
    shares = None
    for tick_index in range(MICRO + 2):

        def first_section():
            send_ahead = zero_send
            kept_now = zero_kept
            if tick_index < MICRO:
                kept_now, send_ahead = encoder_pass(
                    rows_of(enc_input, tick_index), rows_of(key_allowed, tick_index), weights
                )
            enc_grad = zero_enc
            grads = zero_grads
            if tick_index >= 2:
                enc_grad, grads = encoder_back(
                    stored[tick_index - 2], rows_of(key_allowed, tick_index - 2), weights, returned
                )
            return (send_ahead, zero_send, grads, enc_grad, zero_dec, zero_dec, kept_now)

        def second_section():
            if 1 <= tick_index <= MICRO:
                step_index = tick_index - 1
                out_block, dec_grad, send_back, grads = decoder_pass(
                    rows_of(dec_input, step_index),
                    rows_of(out_grad, step_index),
                    arrived,
                    rows_of(self_allowed, step_index),
                    rows_of(key_allowed, step_index),
                    weights,
                )
                return (zero_send, send_back, grads, zero_enc, out_block, dec_grad, zero_kept)
            return (zero_send, zero_send, zero_grads, zero_enc, zero_dec, zero_dec, zero_kept)

        send_ahead, send_back, grads, enc_grad, out_block, dec_grad, kept_now = lax.cond(
            section_index == 0, first_section, second_section
        )
        if tick_index < MICRO:
            stored.append(kept_now)
            arrived = from_behind(send_ahead, "section", 1)
        if 1 <= tick_index <= MICRO:
            returned = from_behind(send_back, "section", -1)
            dec_out_blocks.append(out_block)
            dec_grad_blocks.append(dec_grad)
        if tick_index >= 2:
            enc_grad_blocks.append(enc_grad)
        if tick_index >= 1:
            part_sum = lax.psum_scatter(grads, "batch", scatter_dimension=1, tiled=True)
            shares = part_sum if shares is None else jax.tree.map(jnp.add, shares, part_sum)
    whole = jax.tree.map(
        lambda part, own: part.astype(own.dtype),
        lax.all_gather(shortened(shares), "batch", axis=1, tiled=True),
        shares,
    )
    enc_grads = jnp.concatenate(enc_grad_blocks, axis=0)
    dec_outs = jnp.concatenate(dec_out_blocks, axis=0)
    dec_grads = jnp.concatenate(dec_grad_blocks, axis=0)
    half_width = model_width // 2
    own_start = section_index * half_width
    other_start = (1 - section_index) * half_width

    def columns(array, start):
        return lax.dynamic_slice_in_dim(array, start, half_width, 2)

    swapped = swapped_2(
        (
            columns(enc_grads, other_start),
            columns(dec_outs, other_start),
            columns(dec_grads, other_start),
        ),
        "section",
        0,
    )
    on_first = section_index == 0
    enc_final = jnp.where(on_first, columns(enc_grads, own_start), swapped[0])
    decoded = jnp.where(on_first, swapped[1], columns(dec_outs, own_start))
    dec_final = jnp.where(on_first, swapped[2], columns(dec_grads, own_start))
    return (
        decoded,
        enc_final,
        dec_final,
        whole[0][None],
        whole[1][None],
        whole[2][None],
        whole[3][None],
        whole[4][None],
        whole[5][None],
        whole[6][None],
    )


def solution(mesh):
    placed = (
        P("batch", None, None),
        P("batch", None, None),
        P("batch", None, None),
        P("section", None, None),
        P("section", None, None),
        P("section", None, None),
        P("section", None, None),
        P("section", None, None),
        P("section", None, None),
        P("section", None, None),
        P("batch"),
        P("batch"),
        P("batch"),
    )
    return jax.shard_map(
        per_device,
        mesh=mesh,
        in_specs=placed,
        out_specs=(
            P("batch", None, "section"),
            P("batch", None, "section"),
            P("batch", None, "section"),
            P("section", None, None),
            P("section", None, None),
            P("section", None, None),
            P("section", None, None),
            P("section", None, None),
            P("section", None, None),
            P("section", None, None),
        ),
        check_vma=False,
    )
```

profile of v0, /device:TPU:0, one launch (start us, length us, event | category | flops | bytes accessed | tf_op | source)
XLA Modules:
  0.0 2091.2 jit_solution(17112457578156399242)
XLA Ops:
  9.4 29.4 %conditional.6 = (bf16[1,228,1536]{2,1,0:T(8,128)(2,1)}, f32[1,228,768]{2,1,0:T(8,128)S(1)}, bf16[1,228,768]{2,1,0:T(8,128)(2,1)S(1)}, bf16[1,228,2304]{2,1,0:T(...) conditional(s32[]{:T(128)} %convert_element_type.1008, ...), branch_computations={%region_0.1_spmd, %region_1.10_spmd} | conditional | flops 3950902528 | bytes 126703096 | solution.py:366
  42.1 61.2 %conditional.7 = (bf16[1,228,1536]{2,1,0:T(8,128)(2,1)}, bf16[1,228,1536]{1,2,0:T(8,128)(2,1)}, f32[768,2304]{1,0:T(8,128)}, f32[768,768]{1,0:T(8,128)}, f32[768...) conditional(s32[]{:T(128)} %convert_element_type.1008, ...), branch_computations={%region_10.35_spmd, %region_35.44_spmd} | conditional | flops 3950902528 | bytes 154154224 | solution.py:366
  103.4 38.9 %collective-permute-start.1 = (bf16[1,228,1536]{2,1,0:T(8,128)(2,1)}, bf16[1,228,1536]{2,1,0:T(8,128)(2,1)S(1)}, u32[]{:S(2)}, u32[]{:S(2)}) collective-permute-start(bf16[1,228,1536]{2,1,0:T(8,128)(2,1)} %get-tuple-element.549), channel_id=1, source_target_pairs={{0,16},{1,17},{2,18},{3,19},{4,20},{5,21},{6,22},{7,23},{8,24},{9,... | collective-permute-start | bytes 2101256 | tf_op jit(solution)/shard_map/ppermute | solution.py:18
  148.0 143.6 %conditional.8 = (bf16[1,228,1536]{2,1,0:T(8,128)(2,1)}, bf16[1,228,1536]{2,1,0:T(8,128)(2,1)}, f32[768,1536]{1,0:T(8,128)}, f32[3,768]{1,0:T(4,128)}, f32[3,768...) conditional(s32[]{:T(128)} %convert_element_type.1008, ...), branch_computations={%region_44.69_spmd, %region_69.97_spmd} | conditional | flops 11920074752 | bytes 374505664 | solution.py:366
  297.2 155.4 %conditional.9 = (bf16[1,228,1536]{2,1,0:T(8,128)(2,1)}, bf16[1,228,1536]{2,1,0:T(8,128)(2,1)}, f32[768,1536]{1,0:T(8,128)}, f32[3,768]{1,0:T(4,128)}, f32[3,768...) conditional(s32[]{:T(128)} %convert_element_type.1008, ...), branch_computations={%region_97.122_spmd, %region_122.150_spmd} | conditional | flops 11920074752 | bytes 374499712 | solution.py:366
  458.4 106.0 %conditional.10 = (bf16[1,228,1536]{1,2,0:T(8,128)(2,1)}, f32[768,2304]{1,0:T(8,128)}, f32[768,768]{1,0:T(8,128)}, f32[768,3072]{1,0:T(8,128)}, f32[3072,768]{1,...) conditional(s32[]{:T(128)} %convert_element_type.1008, ...), branch_computations={%region_150.175_spmd, %region_175.195_spmd} | conditional | flops 7969175040 | bytes 263756320 | solution.py:366
  570.1 98.6 %conditional.11 = (f32[768,1536]{1,0:T(8,128)}, f32[3,768]{1,0:T(4,128)}, f32[3,768]{1,0:T(4,128)}, bf16[1,228,768]{2,0,1:T(2,128)(2,1)}, f32[768,2304]{1,0:T(8,...) conditional(s32[]{:T(128)} %convert_element_type.1008, () %tuple.65, ...), branch_computations={%region_195.196_spmd, %region_196.216_spmd} | conditional | flops 7969176064 | bytes 253151600 | solution.py:366
  694.9 15.6 add_add_fusion.38
  718.5 19.9 add_add_fusion.36
  748.2 20.7 add_add_fusion.37
  782.9 23.4 %reduce-scatter.24.cloned.1.call-done = f32[48,768]{1,0:T(8,128)} async-done(((f32[768,768]{1,0:T(8,128)}), f32[48,768]{1,0:T(8,128)}) %reduce-scatter.24.cloned.1.call-update) | async-done | bytes 147472
  807.9 141.1 %reduce-scatter.30.cloned.1.call-done = f32[96,768]{1,0:T(8,128)} async-done(((f32[1536,768]{1,0:T(8,128)}), f32[96,768]{1,0:T(8,128)}) %reduce-scatter.30.cloned.1.call-update) | async-done | bytes 294928
  950.7 154.3 %reduce-scatter.22.cloned.1.call-done = f32[144,768]{1,0:T(8,128)} async-done(((f32[2304,768]{1,0:T(8,128)}), f32[144,768]{1,0:T(8,128)}) %reduce-scatter.22.cloned.1.call-update) | async-done | bytes 442384
  1106.8 172.7 %reduce-scatter.28.cloned.1.call-done = f32[48,3072]{1,0:T(8,128)} async-done(((f32[768,3072]{1,0:T(8,128)}), f32[48,3072]{1,0:T(8,128)}) %reduce-scatter.28.cloned.1.call-update) | async-done | bytes 589840
  1281.6 174.8 %reduce-scatter.26.cloned.1.call-done = f32[192,768]{1,0:T(8,128)} async-done(((f32[3072,768]{1,0:T(8,128)}), f32[192,768]{1,0:T(8,128)}) %reduce-scatter.26.cloned.1.call-update) | async-done | bytes 589840
  1465.4 116.4 %reduce-scatter.32.cloned.1.call-done = f32[48,3]{1,0:T(8,128)} async-done(((f32[768,3]{1,0:T(8,128)}), f32[48,3]{1,0:T(8,128)}) %reduce-scatter.32.cloned.1.call-update) | async-done | bytes 592
  1582.6 38.8 %all-gather = bf16[16,48,3]{1,2,0:T(4,128)(2,1)S(1)} all-gather(bf16[1,48,3]{1,2,0:T(4,128)(2,1)S(1)} %bitcast.1501), channel_id=1, replica_groups=mesh['section'=2,'batch'=16] {'batch'}, dimensions={0}, use_global_device_ids=true | all-gather | bytes 4896 | tf_op jit(solution)/shard_map/all_gather | solution.py:383
  1622.1 86.0 %reduce-scatter.34.cloned.1.call-done = f32[48,3]{1,0:T(8,128)} async-done(((f32[768,3]{1,0:T(8,128)}), f32[48,3]{1,0:T(8,128)}) %reduce-scatter.34.cloned.1.call-update) | async-done | bytes 592
  1708.9 38.8 %all-gather.1 = bf16[16,48,3]{1,2,0:T(4,128)(2,1)S(1)} all-gather(bf16[1,48,3]{1,2,0:T(4,128)(2,1)S(1)} %bitcast.1502), channel_id=1, replica_groups=mesh['section'=2,'batch'=16] {'batch'}, dimensions={0}, use_global_device_ids=true | all-gather | bytes 4896 | tf_op jit(solution)/shard_map/all_gather | solution.py:383
  1749.7 17.1 all-gather.10.cloned.1.call-done
  1770.1 60.6 %all-gather.16.cloned.1.call-done = bf16[768,1536]{0,1:T(8,128)(2,1)} async-done(((bf16[768,96]{0,1:T(8,128)(2,1)}), bf16[768,1536]{0,1:T(8,128)(2,1)}) %all-gather.16.cloned.1.call-update) | async-done | bytes 2359312 | tf_op jit(solution)/shard_map/all_gather | solution.py:383
  1841.0 63.0 %all-gather.8.cloned.1.call-done = bf16[768,2304]{0,1:T(8,128)(2,1)} async-done(((bf16[768,144]{0,1:T(8,128)(2,1)}), bf16[768,2304]{0,1:T(8,128)(2,1)}) %all-gather.8.cloned.1.call-update) | async-done | bytes 3538960 | tf_op jit(solution)/shard_map/all_gather | solution.py:383
  1917.6 68.3 %all-gather.14.cloned.1.call-done = bf16[3072,768]{0,1:T(8,128)(2,1)} async-done(((bf16[3072,48]{0,1:T(8,128)(2,1)}), bf16[3072,768]{0,1:T(8,128)(2,1)}) %all-gather.14.cloned.1.call-update) | async-done | bytes 4718608 | tf_op jit(solution)/shard_map/all_gather | solution.py:383
  2002.8 64.8 %all-gather.12.cloned.1.call-done = bf16[768,3072]{0,1:T(8,128)(2,1)} async-done(((bf16[768,192]{0,1:T(8,128)(2,1)}), bf16[768,3072]{0,1:T(8,128)(2,1)}) %all-gather.12.cloned.1.call-update) | async-done | bytes 4718608 | tf_op jit(solution)/shard_map/all_gather | solution.py:383
  (945 shorter events, 735.2 us)
Async XLA Ops:
  7.2 799.1 %reduce-scatter.24.cloned.1.call-start = ((), (), s32[]{:S(2)}) async-start(), calls=%async_computation.13 | async-start | bytes 2506752
  38.8 3.3 collective-permute-start
  103.4 41.6 %collective-permute-start.1 = (bf16[1,228,1536]{2,1,0:T(8,128)(2,1)}, bf16[1,228,1536]{2,1,0:T(8,128)(2,1)S(1)}, u32[]{:S(2)}, u32[]{:S(2)}) collective-permute-start(bf16[1,228,1536]{2,1,0:T(8,128)(2,1)} %get-tuple-element.549), channel_id=1, source_target_pairs={{0,16},{1,17},{2,18},{3,19},{4,20},{5,21},{6,22},{7,23},{8,24},{9,... | collective-permute-start | bytes 2101256 | tf_op jit(solution)/shard_map/ppermute | solution.py:18
  143.7 4.2 collective-permute-start.2
  291.6 3.3 collective-permute-start.3
  292.9 4.3 collective-permute-start.4
  452.6 3.3 collective-permute-start.5
  454.0 4.4 collective-permute-start.6
  565.8 4.2 collective-permute-start.8
  675.8 273.1 %reduce-scatter.30.cloned.1.call-start = ((), (), s32[]{:S(2)}) async-start(), calls=%async_computation.16 | async-start | bytes 5013504
  694.8 410.2 %reduce-scatter.22.cloned.1.call-start = ((), (), s32[]{:S(2)}) async-start(), calls=%async_computation.12 | async-start | bytes 7520256
  718.5 561.0 %reduce-scatter.28.cloned.1.call-start = ((), (), s32[]{:S(2)}) async-start(), calls=%async_computation.15 | async-start | bytes 10027008
  748.1 708.2 %reduce-scatter.26.cloned.1.call-start = ((), (), s32[]{:S(2)}) async-start(), calls=%async_computation.14 | async-start | bytes 10027008
  778.6 803.2 %reduce-scatter.32.cloned.1.call-start = ((), (), s32[]{:S(2)}) async-start(), calls=%async_computation.17 | async-start | bytes 417792
  780.0 678.2 %copy-start.185 = (bf16[1,32,768]{2,1,0:T(8,128)(2,1)S(1)}, bf16[1,32,768]{2,1,0:T(8,128)(2,1)}, u32[]{:S(2)}) copy-start(bf16[1,32,768]{2,1,0:T(8,128)(2,1)} %get-tuple-element.548) | copy-start | bytes 147460
  781.0 927.1 %reduce-scatter.34.cloned.1.call-start = ((), (), s32[]{:S(2)}) async-start(), calls=%async_computation.18 | async-start | bytes 417792
  782.8 983.9 %all-gather.10.cloned.1.call-start = ((), (), s32[]{:S(2)}) async-start(), calls=%async_computation.8 | async-start | bytes 1253376 | tf_op jit(solution)/shard_map/all_gather | solution.py:383
  807.9 1022.9 %all-gather.16.cloned.1.call-start = ((), (), s32[]{:S(2)}) async-start(), calls=%async_computation.11 | async-start | bytes 2506752 | tf_op jit(solution)/shard_map/all_gather | solution.py:383
  950.6 953.4 %all-gather.8.cloned.1.call-start = ((), (), s32[]{:S(2)}) async-start(), calls=%async_computation.7 | async-start | bytes 3760128 | tf_op jit(solution)/shard_map/all_gather | solution.py:383
  1106.7 879.1 %all-gather.14.cloned.1.call-start = ((), (), s32[]{:S(2)}) async-start(), calls=%async_computation.10 | async-start | bytes 5013504 | tf_op jit(solution)/shard_map/all_gather | solution.py:383
  1281.3 786.3 %all-gather.12.cloned.1.call-start = ((), (), s32[]{:S(2)}) async-start(), calls=%async_computation.9 | async-start | bytes 5013504 | tf_op jit(solution)/shard_map/all_gather | solution.py:383
  1458.4 5.6 collective-permute-start.10
  1458.5 6.2 collective-permute-start.7
  1463.9 284.5 %collective-permute-start.9 = (bf16[4,228,384]{2,0,1:T(4,128)(2,1)S(1)}, bf16[4,228,384]{2,0,1:T(4,128)(2,1)S(1)}, u32[]{:S(2)}, u32[]{:S(2)}) collective-permute-start(bf16[4,228,384]{2,0,1:T(4,128)(2,1)S(1)} %constant_dynamic-slice_fusion.1), channel_id=1, source_target_pairs={{0,16},{16,0},{1,17},{17,1},{2,18},{18,2},{3,19},{19,3},{4,20},{20... | collective-permute-start | bytes 2101256 | tf_op jit(solution)/shard_map/ppermute | solution.py:26
  (228 other events, 6048.4 us)
Sparse Core Ops, SparseCore 0:
  676.0 130.2 reduce-scatter.23
  812.3 136.6 reduce-scatter.29
  954.3 150.6 reduce-scatter.21
  1110.5 168.9 reduce-scatter.27
  1286.5 169.8 reduce-scatter.25
  1461.5 120.3 reduce-scatter.31
  1587.7 120.3 reduce-scatter.33
  1711.5 55.1 all-gather.9
  1769.5 61.1 all-gather.15
  1834.0 70.0 all-gather.7
  1906.8 78.9 all-gather.13
  1988.5 79.0 all-gather.11
where the time goes:
time: 2110 us; the launch traced here: 2090 us
  waiting for transfers between devices  1160 us (55%)
  local copies, waits for them, and re-layouts  297 us (14%)
  matrix products  237 us (11%)
  other arithmetic  235 us (11%)
  blocking collectives  77.6 us (4%)
  starting transfers between devices  49.5 us (2%)
  loops' own time  24.9 us (1%)
    unnamed x19, waiting for transfers between devices  869 us
    all_gather x5, waiting for transfers between devices, per_device(): lax.all_gather(shortened(shares), 'batch', axis=1, tiled=True)  274 us
    cond x18, local copies, waits for them, and re-layouts, per_device(): lax.cond(section_index == 0, first_section, second_section)  101 us
    dot_general x19, matrix products, weight_product(): jnp.einsum('bld,blf->df', left_side, grad_rows, preferred_element_type=jn...  90.5 us
    all_gather x2, blocking collectives, per_device(): lax.all_gather(shortened(shares), 'batch', axis=1, tiled=True)  77.6 us
    unnamed x82, local copies, waits for them, and re-layouts  76.1 us
    add x7, other arithmetic, per_device(): jax.tree.map(jnp.add, shares, part_sum)  75.6 us
    dot_general x20, matrix products, forward_product(): jnp.einsum('bld,df->blf', left_side, matrix, preferred_element_type=jnp.f...  62.1 us
  transfers between devices with their start and end apart: 23, of which 19 were waited for; matrix products, arithmetic and copies ran while one was open for 8% of the time, Pallas kernels for 0%

commit v1 on v0

--- a/solution.py
+++ b/solution.py
@@ -1,29 +1,280 @@
+import functools
+
 import jax
 import jax.numpy as jnp
 from jax import lax
+from jax.experimental import pallas as pl
+from jax.experimental.pallas import tpu as pltpu
 from jax.sharding import PartitionSpec as P
 
 HEAD_DIM = 64
 PATCHES = 196
-MICRO = 4
-
-
 far_below = -1000000000.0
 epsilon = 1e-06
 
-
-def from_behind(shard, axis, by):
-    size = lax.axis_size(axis)
-    pairs = [(i, i + by) for i in range(size) if 0 <= i + by < size]
-    return lax.ppermute(shard, axis, pairs)
-
-
-def shortened(shard):
-    return jax.tree.map(lambda a: a.astype(jnp.bfloat16) if a.dtype == jnp.float32 else a, shard)
-
-
-def swapped_2(shard, axis, stride):
-    return lax.ppermute(shard, axis, [(i, i ^ 1 << stride) for i in range(lax.axis_size(axis))])
+MESH = pl.DeviceIdType.MESH
+NZ = 4
+
+def place():
+    b = lax.axis_index("batch"); c = lax.axis_index("section")
+    return b % 2, (b // 2) % 2, b // 4, c
+
+def bid(x, y, z):
+    return z * 4 + y * 2 + x
+
+def ar_kernel(pairs, rows, width, g, norms, out, norms_out, acc, res, rx, up, dn, ry, nbuf, lsem, asend, arecv, zsend, zrecv, nsem):
+    x, y, z, c = place()
+    half, block, share = rows // 2, rows // 8, rows // 16
+
+    def dev(x, y, z):
+        return (c, bid(x, y, z))
+
+    across = (dev(1 - x, y, z), dev(x, 1 - y, z))
+    above, below = dev(x, y, z + 1), dev(x, y, z - 1)
+    bit = (x, y)
+
+    barrier = pltpu.get_barrier_semaphore()
+    faraway = dev(x, y, (z + 2) % NZ)
+    for d in across + (faraway,):
+        pl.semaphore_signal(barrier, inc=1, device_id=d, device_id_type=MESH)
+
+    @pl.when(z < NZ - 1)
+    def _():
+        pl.semaphore_signal(barrier, inc=1, device_id=above, device_id_type=MESH)
+
+    @pl.when(z > 0)
+    def _():
+        pl.semaphore_signal(barrier, inc=1, device_id=below, device_id_type=MESH)
+
+    pl.semaphore_wait(barrier, 3 + (z + NZ - 1) // NZ + (2 * NZ - 2 - z) // NZ)
+
+    def rdma(src, dst, send, recv, device):
+        return pltpu.make_async_remote_copy(src_ref=src, dst_ref=dst, send_sem=send, recv_sem=recv, device_id=device, device_id_type=MESH)
+
+    def parts(t, f):
+        p = 2 * t + f
+        a, b = bit[f], bit[1 - f]
+        own = a * half
+        other = (1 - a) * half
+        return p, own, other, b
+
+    def rows_at(start, n):
+        return pl.ds(pl.multiple_of(start, 16), n)
+
+    def own_load(t, f):
+        p, own, other, b = parts(t, f)
+        return pltpu.make_async_copy(g.at[p, rows_at(own, half)], acc.at[p], lsem.at[p, 0])
+
+    def own_store(t, f, k):
+        p, own, other, b = parts(t, f)
+        start = own if k == 0 else other
+        return pltpu.make_async_copy(res.at[p, rows_at(start, half)], out.at[p, rows_at(start, half)], lsem.at[p, k + 1])
+
+    def rs_a(t, f):
+        p, own, other, b = parts(t, f)
+        return rdma(g.at[p, rows_at(other, half)], rx.at[p], asend.at[p, 0], arecv.at[p, 0], across[f])
+
+    def rs_up(t, f, k):
+        p, own, other, b = parts(t, f)
+        return rdma(acc.at[p, pl.ds(k * block, block)], up.at[p, k], zsend.at[p, 0, k], zrecv.at[p, 0, k], above)
+
+    def rs_dn(t, f, k):
+        p, own, other, b = parts(t, f)
+        return rdma(acc.at[p, pl.ds(k * block, block)], dn.at[p, k], zsend.at[p, 1, k], zrecv.at[p, 1, k], below)
+
+    def rs_b(t, f):
+        p, own, other, b = parts(t, f)
+        return rdma(acc.at[p, rows_at(z * block + (1 - b) * share, share)], ry.at[p], asend.at[p, 1], arecv.at[p, 1], across[1 - f])
+
+    def ag_b(t, f):
+        p, own, other, b = parts(t, f)
+        s = res.at[p, rows_at(own + z * block + b * share, share)]
+        return rdma(s, s, asend.at[p, 2], arecv.at[p, 2], across[1 - f])
+
+    def ag_up(t, f, k):
+        p, own, other, b = parts(t, f)
+        s = res.at[p, rows_at(own + k * block, block)]
+        return rdma(s, s, zsend.at[p, 2, k], zrecv.at[p, 2, k], above)
+
+    def ag_dn(t, f, k):
+        p, own, other, b = parts(t, f)
+        s = res.at[p, rows_at(own + k * block, block)]
+        return rdma(s, s, zsend.at[p, 3, k], zrecv.at[p, 3, k], below)
+
+    def ag_a(t, f):
+        p, own, other, b = parts(t, f)
+        s = res.at[p, rows_at(own, half)]
+        return rdma(s, s, asend.at[p, 3], arecv.at[p, 3], across[f])
+
+    def s0(t, f):
+        rs_a(t, f).start()
+        own_load(t, f).start()
+
+    def s1(t, f):
+        p, own, other, b = parts(t, f)
+        own_load(t, f).wait()
+        rs_a(t, f).wait()
+        acc[p] = acc[p] + rx[p]
+
+        @pl.when(z == 0)
+        def _():
+            for k in range(NZ - 1, 0, -1):
+                rs_up(t, f, k).start()
+
+        @pl.when(z == NZ - 1)
+        def _():
+            for k in range(NZ - 1):
+                rs_dn(t, f, k).start()
+
+    def chain(t, f, j):
+        p, own, other, b = parts(t, f)
+
+        @pl.when(z == j)
+        def _():
+            for k in range(NZ - 1, j - 1, -1):
+                rs_up(t, f, k).wait_recv()
+                r = pl.ds(k * block, block)
+                acc[p, r] = acc[p, r] + up[p, k]
+                if k > j:
+                    rs_up(t, f, k).start()
+
+        @pl.when(z == NZ - 1 - j)
+        def _():
+            for k in range(NZ - j):
+                rs_dn(t, f, k).wait_recv()
+                r = pl.ds(k * block, block)
+                acc[p, r] = acc[p, r] + dn[p, k]
+                if k < NZ - 1 - j:
+                    rs_dn(t, f, k).start()
+
+    def s4(t, f):
+        chain(t, f, NZ - 1)
+        rs_b(t, f).start()
+
+    def s5(t, f):
+        p, own, other, b = parts(t, f)
+        rs_b(t, f).wait()
+        mine = z * block + b * share
+        res[p, rows_at(own + mine, share)] = acc[p, rows_at(mine, share)] + ry[p]
+        ag_b(t, f).start()
+
+    def s6(t, f):
+        ag_b(t, f).wait()
+
+        @pl.when(z < NZ - 1)
+        def _():
+            ag_up(t, f, z).start()
+
+        @pl.when(z > 0)
+        def _():
+            ag_dn(t, f, z).start()
+
+    def spread(t, f, j):
+        @pl.when(z >= j)
+        def _():
+            ag_up(t, f, z - j).wait_recv()
+
+            @pl.when(z < NZ - 1)
+            def _():
+                ag_up(t, f, z - j).start()
+
+        @pl.when(z + j <= NZ - 1)
+        def _():
+            ag_dn(t, f, z + j).wait_recv()
+
+            @pl.when(z > 0)
+            def _():
+                ag_dn(t, f, z + j).start()
+
+    def s9(t, f):
+        spread(t, f, NZ - 1)
+        ag_a(t, f).start()
+        own_store(t, f, 0).start()
+
+    def s10(t, f):
+        ag_a(t, f).wait()
+        own_store(t, f, 1).start()
+        for k in range(NZ):
+            @pl.when((z < k))
+            def _(k=k):
+                rs_up(t, f, k).wait_send()
+
+            @pl.when((z > k))
+            def _(k=k):
+                rs_dn(t, f, k).wait_send()
+
+            @pl.when((k <= z) & (z < NZ - 1))
+            def _(k=k):
+                ag_up(t, f, k).wait_send()
+
+            @pl.when((k >= z) & (z > 0))
+            def _(k=k):
+                ag_dn(t, f, k).wait_send()
+
+    def s11(t, f):
+        own_store(t, f, 0).wait()
+        own_store(t, f, 1).wait()
+
+    mates = across + (dev(x, y, z + 1 - 2 * (z % 2)), faraway)
+
+    def norm_swap(j):
+        return rdma(norms_out, nbuf.at[j], nsem.at[0, j], nsem.at[1, j], mates[j])
+
+    norms_out[...] = norms[...]
+    norm_swap(0).start()
+
+    stages = [s0, s1] + [functools.partial(lambda j, t, f: chain(t, f, j), j) for j in range(1, NZ - 1)] + [s4, s5, s6] + [
+        functools.partial(lambda j, t, f: spread(t, f, j), j) for j in range(1, NZ - 1)] + [s9, s10, s11]
+    ahead = 2
+
+    def tick(tau, carry):
+        for j in range(4):
+
+            @pl.when(tau == 3 * j + 3)
+            def _(j=j):
+                norm_swap(j).wait()
+                norms_out[...] = norms_out[...] + nbuf[j]
+                if j < 3:
+                    norm_swap(j + 1).start()
+
+        for i, stage in enumerate(stages):
+            lag = 0 if i == 0 else i - 1 + ahead
+            t = tau - lag
+
+            @pl.when((t >= 0) & (t < pairs))
+            def _(stage=stage, t=t):
+                stage(t, 0)
+                stage(t, 1)
+        return carry
+    lax.fori_loop(0, pairs + len(stages) - 2 + ahead, tick, 0)
+
+
+def all_reduce(g, norms, collective_id):
+    n, rows, width = g.shape
+    half, block, share = rows // 2, rows // 8, rows // 16
+    bf = jnp.bfloat16
+    return pl.pallas_call(
+        functools.partial(ar_kernel, n // 2, rows, width),
+        out_shape=(jax.ShapeDtypeStruct((n, rows, width), bf), jax.ShapeDtypeStruct(norms.shape, norms.dtype)),
+        in_specs=[pl.BlockSpec(memory_space=pl.ANY), pl.BlockSpec(memory_space=pltpu.VMEM)],
+        out_specs=(pl.BlockSpec(memory_space=pl.ANY), pl.BlockSpec(memory_space=pltpu.VMEM)),
+        scratch_shapes=[
+            pltpu.VMEM((n, half, width), bf),
+            pltpu.VMEM((n, rows, width), bf),
+            pltpu.VMEM((n, half, width), bf),
+            pltpu.VMEM((n, NZ, block, width), bf),
+            pltpu.VMEM((n, NZ, block, width), bf),
+            pltpu.VMEM((n, share, width), bf),
+            pltpu.VMEM((4,) + norms.shape, norms.dtype),
+            pltpu.SemaphoreType.DMA((n, 3)),
+            pltpu.SemaphoreType.DMA((n, 4)),
+            pltpu.SemaphoreType.DMA((n, 4)),
+            pltpu.SemaphoreType.DMA((n, 4, NZ)),
+            pltpu.SemaphoreType.DMA((n, 4, NZ)),
+            pltpu.SemaphoreType.DMA((2, 4)),
+        ],
+        compiler_params=pltpu.CompilerParams(collective_id=collective_id, has_side_effects=True, vmem_limit_bytes=60 * 2**20),
+    )(g, norms)
 
 
 def layer_norm(inputs, gain_row, shift_row):
@@ -165,25 +416,6 @@
     return ((inputs, kept_attention, hidden, kept_forward, result, memory), keys_values)
 
 
-def zero_encoder_kept(items, enc_len, model_width, hidden_units):
-    heads = model_width // HEAD_DIM
-    wide_float = jnp.zeros((items, enc_len, model_width), jnp.float32)
-    wide_low = jnp.zeros((items, enc_len, model_width), jnp.bfloat16)
-    kept_attention = (
-        wide_low,
-        jnp.zeros((items, enc_len, 3 * model_width), jnp.bfloat16),
-        wide_low,
-        jnp.zeros((items, heads, enc_len, 1), jnp.float32),
-    )
-    kept_forward = (
-        wide_low,
-        jnp.zeros((items, enc_len, hidden_units), jnp.float32),
-        jnp.zeros((items, enc_len, hidden_units), jnp.bfloat16),
-        wide_float,
-    )
-    return (wide_float, kept_attention, wide_float, kept_forward, wide_float, wide_low)
-
-
 def encoder_back(kept, allowed, weights, grad_keys_values):
     qkv_matrix, out_matrix, up_matrix, down_matrix, cross_matrix, gains, shifts = weights
     inputs, kept_attention, hidden, kept_forward, result, memory = kept
@@ -280,6 +512,23 @@
     return (positions[None, None, :] <= positions[None, :, None]) & (
         positions[None, None, :] < suffix_rows[:, None, None]
     )
+
+
+WIDTH = 256
+
+
+def to_panels(matrix):
+    rows, columns = matrix.shape
+    high = 768
+    split = matrix.reshape(rows // high, high, columns // WIDTH, WIDTH)
+    return split.transpose(0, 2, 1, 3).reshape(-1, high, WIDTH)
+
+
+def from_panels(panels, shape):
+    rows, columns = shape
+    high = panels.shape[1]
+    split = panels.reshape(rows // high, columns // WIDTH, high, WIDTH)
+    return split.transpose(0, 2, 1, 3).reshape(shape).astype(jnp.float32)
 
 
 def per_device(
@@ -297,13 +546,9 @@
     prefix_len,
     suffix_len,
 ):
-    section_index = lax.axis_index("section")
-    items_dev = enc_input.shape[0]
-    per_step = items_dev // MICRO
-    enc_len = enc_input.shape[1]
+    section = lax.axis_index("section")
+    items, enc_len, model_width = enc_input.shape
     dec_len = dec_input.shape[1]
-    model_width = enc_input.shape[2]
-    hidden_units = mlp_in.shape[2]
     weights = (
         attn_qkv[0],
         attn_out[0],
@@ -313,144 +558,90 @@
         norm_gain[0].astype(jnp.float32),
         norm_shift[0].astype(jnp.float32),
     )
-    has_image = jnp.arange(items_dev, dtype=jnp.int32) < image_count[0]
+    has_image = jnp.arange(items, dtype=jnp.int32) < image_count[0]
     key_allowed = encoder_keys(has_image, prefix_len, enc_len)
     self_allowed = decoder_mask(suffix_len, dec_len)
-    zero_send = jnp.zeros((per_step, enc_len, 2 * model_width), jnp.bfloat16)
-    zero_enc = jnp.zeros((per_step, enc_len, model_width), jnp.bfloat16)
-    zero_dec = jnp.zeros((per_step, dec_len, model_width), jnp.bfloat16)
-    zero_grads = tuple((jnp.zeros(matrix.shape, jnp.float32) for matrix in weights))
-    zero_kept = zero_encoder_kept(per_step, enc_len, model_width, hidden_units)
-
-    def rows_of(array, step_index):
-        return array[step_index * per_step : (step_index + 1) * per_step]
-
-    arrived = zero_send
-    returned = zero_send
-    stored = []
-    enc_grad_blocks = []
-    dec_out_blocks = []
-    dec_grad_blocks = []
-    shares = None
-    for tick_index in range(MICRO + 2):
-
-        def first_section():
-            send_ahead = zero_send
-            kept_now = zero_kept
-            if tick_index < MICRO:
-                kept_now, send_ahead = encoder_pass(
-                    rows_of(enc_input, tick_index), rows_of(key_allowed, tick_index), weights
-                )
-            enc_grad = zero_enc
-            grads = zero_grads
-            if tick_index >= 2:
-                enc_grad, grads = encoder_back(
-                    stored[tick_index - 2], rows_of(key_allowed, tick_index - 2), weights, returned
-                )
-            return (send_ahead, zero_send, grads, enc_grad, zero_dec, zero_dec, kept_now)
-
-        def second_section():
-            if 1 <= tick_index <= MICRO:
-                step_index = tick_index - 1
-                out_block, dec_grad, send_back, grads = decoder_pass(
-                    rows_of(dec_input, step_index),
-                    rows_of(out_grad, step_index),
-                    arrived,
-                    rows_of(self_allowed, step_index),
-                    rows_of(key_allowed, step_index),
-                    weights,
-                )
-                return (zero_send, send_back, grads, zero_enc, out_block, dec_grad, zero_kept)
-            return (zero_send, zero_send, zero_grads, zero_enc, zero_dec, zero_dec, zero_kept)
-
-        send_ahead, send_back, grads, enc_grad, out_block, dec_grad, kept_now = lax.cond(
-            section_index == 0, first_section, second_section
+
+    def blank(function, *args):
+        return jax.tree.map(
+            lambda a: jnp.zeros(a.shape, a.dtype), jax.eval_shape(function, *args)
         )
-        if tick_index < MICRO:
-            stored.append(kept_now)
-            arrived = from_behind(send_ahead, "section", 1)
-        if 1 <= tick_index <= MICRO:
-            returned = from_behind(send_back, "section", -1)
-            dec_out_blocks.append(out_block)
-            dec_grad_blocks.append(dec_grad)
-        if tick_index >= 2:
-            enc_grad_blocks.append(enc_grad)
-        if tick_index >= 1:
-            part_sum = lax.psum_scatter(grads, "batch", scatter_dimension=1, tiled=True)
-            shares = part_sum if shares is None else jax.tree.map(jnp.add, shares, part_sum)
-    whole = jax.tree.map(
-        lambda part, own: part.astype(own.dtype),
-        lax.all_gather(shortened(shares), "batch", axis=1, tiled=True),
-        shares,
-    )
-    enc_grads = jnp.concatenate(enc_grad_blocks, axis=0)
-    dec_outs = jnp.concatenate(dec_out_blocks, axis=0)
-    dec_grads = jnp.concatenate(dec_grad_blocks, axis=0)
-    half_width = model_width // 2
-    own_start = section_index * half_width
-    other_start = (1 - section_index) * half_width
+
+    def on_section(wanted, function, *args):
+        return lax.cond(
+            section == wanted, lambda: function(*args), lambda: blank(function, *args)
+        )
+
+    def packed(grads):
+        panels = [to_panels(g.astype(jnp.bfloat16)) for g in grads[:5]]
+        return jnp.concatenate(panels, axis=0), jnp.concatenate(
+            [grads[5], grads[6], jnp.zeros((2, model_width), jnp.float32)], axis=0
+        )
+
+    kept, keys_values = on_section(
+        0, lambda: encoder_pass(enc_input, key_allowed, weights)
+    )
+    arrived = lax.ppermute(keys_values, "section", [(0, 1)])
+
+    def decode():
+        out, grad, back, grads = decoder_pass(
+            dec_input, out_grad, arrived, self_allowed, key_allowed, weights
+        )
+        return out, grad, back, packed(grads)
+
+    dec_out, dec_grad, send_back, dec_packed = on_section(1, decode)
+    returned = lax.ppermute(send_back, "section", [(1, 0)])
+
+    def encode_back():
+        grad, grads = encoder_back(kept, key_allowed, weights, returned)
+        return grad, packed(grads)
+
+    enc_grad, own_packed = lax.cond(
+        section == 0, encode_back, lambda: (blank(encode_back)[0], dec_packed)
+    )
+    panels, norms = own_packed
+    if lax.axis_size("batch") == 16:
+        panels, norms = all_reduce(panels, norms, 0)
+    else:
+        panels = lax.psum(panels, "batch")
+        norms = lax.psum(norms, "batch")
+    grads = []
+    first = 0
+    for matrix in weights[:5]:
+        count = matrix.size // (768 * WIDTH)
+        grads.append(from_panels(panels[first : first + count], matrix.shape)[None])
+        first += count
+    half = model_width // 2
 
     def columns(array, start):
-        return lax.dynamic_slice_in_dim(array, start, half_width, 2)
-
-    swapped = swapped_2(
-        (
-            columns(enc_grads, other_start),
-            columns(dec_outs, other_start),
-            columns(dec_grads, other_start),
-        ),
+        return lax.dynamic_slice_in_dim(array, start, half, 2)
+
+    on_first = section == 0
+    swap = [(0, 1), (1, 0)]
+    own_start, other_start = section * half, (1 - section) * half
+    enc_theirs, out_theirs, dec_theirs = lax.ppermute(
+        (columns(enc_grad, other_start), columns(dec_out, other_start), columns(dec_grad, other_start)),
         "section",
-        0,
-    )
-    on_first = section_index == 0
-    enc_final = jnp.where(on_first, columns(enc_grads, own_start), swapped[0])
-    decoded = jnp.where(on_first, swapped[1], columns(dec_outs, own_start))
-    dec_final = jnp.where(on_first, swapped[2], columns(dec_grads, own_start))
+        swap,
+    )
     return (
-        decoded,
-        enc_final,
-        dec_final,
-        whole[0][None],
-        whole[1][None],
-        whole[2][None],
-        whole[3][None],
-        whole[4][None],
-        whole[5][None],
-        whole[6][None],
+        jnp.where(on_first, out_theirs, columns(dec_out, own_start)),
+        jnp.where(on_first, columns(enc_grad, own_start), enc_theirs),
+        jnp.where(on_first, dec_theirs, columns(dec_grad, own_start)),
+        *grads,
+        norms[None, :3],
+        norms[None, 3:6],
     )
 
 
 def solution(mesh):
-    placed = (
-        P("batch", None, None),
-        P("batch", None, None),
-        P("batch", None, None),
-        P("section", None, None),
-        P("section", None, None),
-        P("section", None, None),
-        P("section", None, None),
-        P("section", None, None),
-        P("section", None, None),
-        P("section", None, None),
-        P("batch"),
-        P("batch"),
-        P("batch"),
-    )
+    items = P("batch", None, None)
+    matrix = P("section", None, None)
+    halves = P("batch", None, "section")
     return jax.shard_map(
         per_device,
         mesh=mesh,
-        in_specs=placed,
-        out_specs=(
-            P("batch", None, "section"),
-            P("batch", None, "section"),
-            P("batch", None, "section"),
-            P("section", None, None),
-            P("section", None, None),
-            P("section", None, None),
-            P("section", None, None),
-            P("section", None, None),
-            P("section", None, None),
-            P("section", None, None),
-        ),
+        in_specs=(items,) * 3 + (matrix,) * 7 + (P("batch"),) * 3,
+        out_specs=(halves,) * 3 + (matrix,) * 7,
         check_vma=False,
     )

time: 2110 us -> 742 us (0.35)
  waiting for transfers between devices: 1160 us -> 4.86 us
  other arithmetic: 235 us -> 72.8 us
  Pallas kernels: 0 us -> 149 us
  starting transfers between devices: 49.5 us -> 158 us
  local copies, waits for them, and re-layouts: 297 us -> 198 us
  matrix products: 237 us -> 145 us
  blocking collectives: 77.6 us -> 0 us
    unnamed x19 -> x0, waiting for transfers between devices: 869 us -> none
    all_gather x5 -> x0, waiting for transfers between devices: 274 us -> none  [per_device(): lax.all_gather(shortened(shares), 'batch', axis=1, tiled=True)]
    pallas_call x0 -> x1, Pallas kernels: none -> 149 us  [all_reduce(): pl.pallas_call(functools.partial(ar_kernel, n // 2, rows, width), out_sha...]
    ppermute x11 -> x5, starting transfers between devices: 48.8 us -> 158 us  [the longest x3 154 us: per_device(): lax.ppermute((columns(enc_grad, other_start), columns(dec_out, other_star...]
    add x11 -> x0, other arithmetic: 80 us -> none  [the longest x7 75.6 us: per_device(): jax.tree.map(jnp.add, shares, part_sum)]
    all_gather x2 -> x0, blocking collectives: 77.6 us -> none  [per_device(): lax.all_gather(shortened(shares), 'batch', axis=1, tiled=True)]
    cond x416 -> x76, local copies, waits for them, and re-layouts: 117 us -> 47.3 us  [the longest x2 23.3 us: per_device(): lax.cond(section == 0, encode_back, lambda: (blank(encode_back)[0], dec_p...]
    dot_general x19 -> x5, matrix products: 90.5 us -> 32.3 us  [weight_product(): jnp.einsum('bld,blf->df', left_side, grad_rows, preferred_element_type=jn...]
  transfers between devices with their start and end apart: 23 -> 5, of which waited for: 19 -> 2; matrix products, arithmetic and copies ran while one was open for 8% -> 13% of each run, Pallas kernels for 0% -> 0%
where the time goes in v1:
time: 742 us; the launch traced here: 735 us
  local copies, waits for them, and re-layouts  198 us (27%)
  starting transfers between devices  158 us (21%)
  Pallas kernels  149 us (20%)
  matrix products  145 us (20%)
  other arithmetic  72.8 us (10%)
    ppermute x3, starting transfers between devices, per_device(): lax.ppermute((columns(enc_grad, other_start), columns(dec_out, other_star...  154 us
    pallas_call x1, Pallas kernels, all_reduce(): pl.pallas_call(functools.partial(ar_kernel, n // 2, rows, width), out_sha...  149 us
    convert_element_type x6, local copies, waits for them, and re-layouts, from_panels(): return split.transpose(0, 2, 1, 3).reshape(shape).astype(jnp.float32)  46.8 us
    dot_general x5, matrix products, backward_product(): jnp.einsum('blf,df->bld', grad_rows, matrix, preferred_element_type=jnp.f...  38.2 us
    dot_general x5, matrix products, forward_product(): jnp.einsum('bld,df->blf', left_side, matrix, preferred_element_type=jnp.f...  37.7 us
    unnamed x19, local copies, waits for them, and re-layouts  37.6 us
    dot_general x5, matrix products, weight_product(): jnp.einsum('bld,blf->df', left_side, grad_rows, preferred_element_type=jn...  32.3 us
    cond x2, local copies, waits for them, and re-layouts, per_device(): lax.cond(section == 0, encode_back, lambda: (blank(encode_back)[0], dec_p...  23.3 us
  transfers between devices with their start and end apart: 5, of which 2 were waited for; matrix products, arithmetic and copies ran while one was open for 13% of the time, Pallas kernels for 0%

profile of v1, /device:TPU:0, one launch (start us, length us, event | category | flops | bytes accessed | tf_op | source)
XLA Modules:
  0.0 734.8 jit_solution(14382453198031020276)
XLA Ops:
  2.8 79.5 %conditional.3 = (f32[4,228,768]{2,1,0:T(8,128)S(1)}, bf16[4,228,768]{2,1,0:T(8,128)(2,1)}, bf16[4,228,2304]{2,1,0:T(8,128)(2,1)}, bf16[4,228,768]{1,2,0:T(8,128...) conditional(s32[]{:T(128)} %convert_element_type.313, () %tuple.33, ...), branch_computations={%region_0.1_spmd, %region_1.10_spmd} | conditional | flops 15778395136 | bytes 225591840 | solution.py:571
  8.4 6.8 convolution_convert_fusion
  49.6 11.3 %fusion.7 = (bf16[4,228,3072]{2,1,0:T(8,128)(2,1)}, f32[4,228,3072]{2,1,0:T(8,128)}) fusion(bf16[4,228,768]{2,1,0:T(8,128)(2,1)} %add_convert_fusion.1, bf16[768,3072]{1,0:T(8,128)(2,1)S(1)} %bitcast.361), kind=kOutput, calls=%fused_computation.8 | convolution fusion | flops 4328570880 | bytes 22929408 | tf_op jit(solution)/shard_map/cond/branch_1_fun/bld,df->blf/dot_general | solution.py:298
  60.9 9.8 %fusion.175 = (f32[4,228]{1,0:T(4,128)S(1)}, f32[4,228,768]{2,1,0:T(8,128)}) fusion(f32[4,228,768]{2,1,0:T(8,128)} %get-tuple-element.490, bf16[4,228,3072]{2,1,0:T(8,128)(2,1)} %get-tuple-element.493, bf16[3072,768]{1,0:T(8,128)(2,1)S(1)} %bitcast.383), kind=kOutput, calls=%fused_computation.323 | convolution fusion | flops 4304755712 | bytes 15928896 | tf_op jit(solution)/shard_map/cond/branch_1_fun/bld,df->blf/dot_general | solution.py:298
  93.6 14.2 %conditional.4 = (bf16[4,32,768]{2,1,0:T(8,128)(2,1)}, bf16[4,32,768]{2,1,0:T(8,128)(2,1)}, bf16[4,228,1536]{1,2,0:T(8,128)(2,1)}, bf16[42,768,256]{1,2,0:T(8,128)(2,1)}, f32[8,768]{1,0:T(8,128)}) conditional(s32[]{:T(128)} %convert_element_type.308, () %tuple.32, (bf16[4,32,768]{2,1,0:T(8,128)(2,1)S(1)}, f32[3,768]{1,0:T(4,128)S(1)}, ...), branch_computations={%region_10.11_spmd, %region_11.36_spmd} | conditional | flops 6704268288 | bytes 328360864 | solution.py:571
  115.8 153.9 %collective-permute-start.1 = (bf16[4,32,384]{2,1,0:T(8,128)(2,1)S(1)}, bf16[4,32,384]{2,1,0:T(8,128)(2,1)S(1)}, u32[]{:S(2)}, u32[]{:S(2)}) collective-permute-start(bf16[4,32,384]{2,1,0:T(8,128)(2,1)S(1)} %constant_dynamic-slice_fusion.2), channel_id=1, source_target_pairs={{0,16},{16,0},{1,17},{17,1},{2,18},{18,2},{3,19},{19,3},{4,20},{20... | collective-permute-start | bytes 294920 | tf_op jit(solution)/shard_map/ppermute | solution.py:622
  275.1 180.0 %conditional.5 = (bf16[42,768,256]{1,2,0:T(8,128)(2,1)}, f32[8,768]{1,0:T(8,128)}, bf16[4,228,768]{2,0,1:T(4,128)(2,1)S(1)}) conditional(s32[]{:T(128)} %convert_element_type.313, (bf16[42,768,256]{1,2,0:T(8,128)(2,1)}, f32[8,768]{1,0:T(8,128)}) %tuple.36, (bf16[4,228,1536]{2,0,1:T(4,128)(2,1)}, bf16[768,1536]{1,0:T(8,128)(2,1)}, ...), branch_computations={%region_36.37_spmd, %region_37.57_spmd} | conditional | flops 31904808960 | bytes 577937920 | solution.py:599
  291.5 14.6 %fusion.133 = bf16[4,228,3072]{2,1,0:T(8,128)(2,1)} fusion(f32[4,228,3072]{2,1,0:T(8,128)} %get-tuple-element.129, bf16[3072,768]{1,0:T(8,128)(2,1)S(1)} %bitcast.385, f32[4,228,768]{2,1,0:T(8,128)S(1)} %get-tuple-element.415, f32[4,228]{1,0:T(4,128)S(1)} %negate_multiply_fusion.5), kind=kOutput, calls=%fused_computation.221 | convolution fusion | flops 4360790016 | bytes 24333888 | tf_op jit(solution)/shard_map/cond/branch_1_fun/blf,df->bld/dot_general | solution.py:302
  306.1 8.7 %multiply_reduce_fusion.13 = (f32[768]{0:T(1024)S(1)}, f32[4,228]{1,0:T(4,128)S(1)}, f32[768]{0:T(1024)S(1)}, f32[4,228,768]{2,1,0:T(8,128)S(1)}) fusion(f32[4,228,768]{2,1,0:T(8,128)} %get-tuple-element.131, f32[4,228]{1,0:T(4,128)S(1)} %fusion.161, f32[4,228]{1,0:T(4,128)S(1)} %broadcast_multiply_fusion.7, f32[768]{0:T(1024)S(1)} %get-tuple-element.408, ...), kind=kOutput, calls=%fused_computation.249 | convolution fusion | flops 4308956160 | bytes 15945408 | tf_op jit(solution)/shard_map/cond/branch_1_fun/blf,df->bld/dot_general | solution.py:302
  344.5 13.6 %multiply_reduce_fusion.11 = (f32[4,12,228]{2,1,0:T(8,128)S(1)}, f32[4,12,228,228]{2,3,1,0:T(8,128)}) fusion(f32[4,12,228,228]{2,3,1,0:T(8,128)} %copy-done, f32[4,12,228]{2,1,0:T(8,128)S(1)} %bitcast.374, pred[4,228]{1,0:T(4,128)(4,1)S(1)} %get-tuple-element.132, bf16[4,228,12,64]{1,3,2,0:T(8,128)(2,1)} %bitcast.351, bf16[4,228,12,64]{1,3,2,0:T(8,128)(2,1)} %bitcast.350), kind=kOutput, calls=%fused_computation.223 | convolution fusion | flops 331854912 | bytes 22851984 | tf_op jit(solution)/shard_map/cond/branch_1_fun/bqhe,bkhe->bhqk/dot_general | solution.py:337
  358.1 7.5 %multiply_convert_fusion.6 = bf16[4,12,228,228]{2,3,1,0:T(8,128)(2,1)S(1)} fusion(f32[4,12,228,228]{2,3,1,0:T(8,128)} %get-tuple-element.440, f32[4,12,228,228]{2,3,1,0:T(8,128)S(1)} %bitcast.319, f32[4,12,228]{2,1,0:T(8,128)S(1)} %get-tuple-element.439, f32[4,12,228]{2,1,0:T(8,128)S(1)} %bitcast.375, pred[4,228]{1,0:T(4,128)(4,1)S(1)} %get-tuple-element.132), kind=kLoop, calls=%fused_computation.222 | loop fusion | flops 14971392 | bytes 25040784 | tf_op jit(solution)/shard_map/cond/branch_1_fun/convert_element_type | solution.py:347
  392.2 6.8 bitcast_convert_fusion.7
  402.0 9.5 %fusion.145 = bf16[3072,768]{0,1:T(8,128)(2,1)} fusion(bf16[4,228,3072]{2,1,0:T(8,128)(2,1)} %get-tuple-element.141, f32[4,228,768]{2,1,0:T(8,128)S(1)} %copy-done.8, f32[4,228]{1,0:T(4,128)S(1)} %negate_multiply_fusion.5), kind=kOutput, calls=%fused_computation.239 | convolution fusion | flops 4307116032 | bytes 13127232 | tf_op jit(solution)/shard_map/cond/branch_1_fun/bld,blf->df/dot_general | solution.py:306
  411.5 9.9 %reshape.585 = bf16[4,768,3,256]{1,0,3,2:T(4,128)(2,1)} reshape(bf16[3072,768]{0,1:T(8,128)(2,1)} %fusion.145) | data formatting | bytes 9437184 | tf_op jit(solution)/shard_map/cond/branch_1_fun/reshape | solution.py:523
  455.1 22.8 %copy.181.g = bf16[42,768,256]{2,1,0:T(8,128)(2,1)} copy(bf16[42,768,256]{1,2,0:T(8,128)(2,1)} %get-tuple-element.193) | data formatting | bytes 33030144 | tf_op jit(solution)/shard_map/cond | solution.py:599
  477.8 149.2 %shard_map.208 = (bf16[42,768,256]{2,1,0:T(8,128)(2,1)}, f32[8,768]{1,0:T(8,128)}) custom-call(bf16[42,768,256]{2,1,0:T(8,128)(2,1)} %copy.181.g, f32[8,768]{1,0:T(8,128)} %get-tuple-element.194.norms), custom_call_target="tpu_custom_call" | custom-call | tf_op jit(solution)/shard_map/pallas_call | solution.py:256
  632.7 10.2 %fusion.183 = (bf16[12,768,256]{2,1,0:T(8,128)(2,1)}, f32[1,768,12,256]{3,1,2,0:T(8,128)}) fusion(bf16[42,768,256]{2,1,0:T(8,128)(2,1)} %get-tuple-element.195), kind=kLoop, calls=%fused_computation.331 | loop fusion | flops 2359296 | bytes 23592960 | tf_op jit(solution)/shard_map/slice | solution.py:612
  644.7 8.0 %copy.182 = f32[1,768,9,256]{1,3,2,0:T(8,128)} copy(f32[1,768,9,256]{3,1,2,0:T(8,128)} %convert_bitcast_fusion.1) | data formatting | bytes 14155776 | tf_op jit(solution)/shard_map/convert_element_type | solution.py:531
  652.7 8.0 %copy.187 = f32[1,768,2304]{2,1,0:T(8,128)} copy(f32[1,768,2304]{1,2,0:T(8,128)} %bitcast.322) | data formatting | bytes 14155776
  665.6 9.6 %copy.184 = f32[1,768,12,256]{1,3,2,0:T(8,128)} copy(f32[1,768,12,256]{3,1,2,0:T(8,128)} %get-tuple-element.468) | data formatting | bytes 18874368 | tf_op jit(solution)/shard_map/convert_element_type | solution.py:531
  675.3 9.6 %copy.189 = f32[1,768,3072]{2,1,0:T(8,128)} copy(f32[1,768,3072]{1,2,0:T(8,128)} %bitcast.320) | data formatting | bytes 18874368
  684.8 8.9 %copy.185 = f32[4,3,768,256]{2,0,3,1:T(4,128)} copy(bf16[4,3,768,256]{3,2,1,0:T(8,128)(2,1)} %bitcast.330) | data formatting | bytes 14155776 | tf_op jit(solution)/shard_map/convert_element_type | solution.py:531
  693.8 12.3 %reshape.594 = f32[1,3072,768]{1,2,0:T(8,128)} reshape(f32[4,768,3,256]{1,0,3,2:T(4,128)} %bitcast.321) | data formatting | bytes 18874368 | tf_op jit(solution)/shard_map/convert_element_type | solution.py:531
  706.1 9.6 %copy.190 = f32[1,3072,768]{2,1,0:T(8,128)} copy(f32[1,3072,768]{1,2,0:T(8,128)} %reshape.594) | data formatting | bytes 18874368
  (203 shorter events, 226.7 us)
Async XLA Ops:
  4.9 34.4 %copy-start.1 = (f32[4,228,768]{2,1,0:T(8,128)}, f32[4,228,768]{2,1,0:T(8,128)S(1)}, u32[]{:S(2)}) copy-start(f32[4,228,768]{2,1,0:T(8,128)S(1)} %get-tuple-element.485) | copy-start | bytes 8404996 | tf_op jit(solution)/shard_map/cond
  32.1 17.5 %slice-start.3 = ((s8[4718592]{0:T(1024)(128)(4,1)}), s8[4194304]{0:T(1024)(128)(4,1)S(1)}, s32[]{:S(2)}) async-start(s8[4718592]{0:T(1024)(128)(4,1)} %bitcast.360), calls=%async_computation.3 | async-start | bytes 8388608 | tf_op jit(solution)/shard_map/cond
  35.3 14.2 %slice-start.4 = ((s8[4718592]{0:T(1024)(128)(4,1)}), s8[524288]{0:T(1024)(128)(4,1)S(1)}, s32[]{:S(2)}) async-start(s8[4718592]{0:T(1024)(128)(4,1)} %bitcast.360), calls=%async_computation.4 | async-start | bytes 1048576 | tf_op jit(solution)/shard_map/cond
  45.9 14.9 %slice-start.9 = ((s8[4718592]{0:T(1024)(128)(4,1)}), s8[4194304]{0:T(1024)(128)(4,1)S(1)}, s32[]{:S(2)}) async-start(s8[4718592]{0:T(1024)(128)(4,1)} %bitcast.382), calls=%async_computation.9 | async-start | bytes 8388608 | tf_op jit(solution)/shard_map/cond
  49.6 11.3 %slice-start.10 = ((s8[4718592]{0:T(1024)(128)(4,1)}), s8[524288]{0:T(1024)(128)(4,1)S(1)}, s32[]{:S(2)}) async-start(s8[4718592]{0:T(1024)(128)(4,1)} %bitcast.382), calls=%async_computation.10 | async-start | bytes 1048576 | tf_op jit(solution)/shard_map/cond
  82.3 11.3 %copy-start.22 = (bf16[4,32,768]{2,1,0:T(8,128)(2,1)S(1)}, bf16[4,32,768]{2,1,0:T(8,128)(2,1)}, u32[]{:S(2)}) copy-start(bf16[4,32,768]{2,1,0:T(8,128)(2,1)} %param.20) | copy-start | bytes 589828
  82.3 11.3 %copy-start.78 = (s32[4]{0:T(128)S(1)}, s32[4]{0:T(128)}, u32[]{:S(2)}) copy-start(s32[4]{0:T(128)} %param.31) | copy-start | bytes 52
  87.1 6.4 collective-permute-start
  107.7 167.3 %copy-start.55 = (f32[4,12,228,1]{2,1,0,3:T(8,128)S(1)}, f32[4,12,228,1]{2,1,0,3:T(8,128)}, u32[]{:S(2)}) copy-start(f32[4,12,228,1]{2,1,0,3:T(8,128)} %get-tuple-element.184) | copy-start | bytes 131332
  113.6 161.5 %collective-permute-start.2 = (bf16[4,228,1536]{2,0,1:T(4,128)(2,1)}, bf16[4,228,1536]{2,0,1:T(4,128)(2,1)}, u32[]{:S(2)}, u32[]{:S(2)}) collective-permute-start(bf16[4,228,1536]{2,0,1:T(4,128)(2,1)} %copy.175), channel_id=1, source_target_pairs={{16,0},{17,1},{18,2},{19,3},{20,4},{21,5},{22,6},{23,7},{24,8},{25... | collective-permute-start | bytes 8405000 | tf_op jit(solution)/shard_map/ppermute | solution.py:593
  115.8 156.2 %collective-permute-start.1 = (bf16[4,32,384]{2,1,0:T(8,128)(2,1)S(1)}, bf16[4,32,384]{2,1,0:T(8,128)(2,1)S(1)}, u32[]{:S(2)}, u32[]{:S(2)}) collective-permute-start(bf16[4,32,384]{2,1,0:T(8,128)(2,1)S(1)} %constant_dynamic-slice_fusion.2), channel_id=1, source_target_pairs={{0,16},{16,0},{1,17},{17,1},{2,18},{18,2},{3,19},{19,3},{4,20},{20... | collective-permute-start | bytes 294920 | tf_op jit(solution)/shard_map/ppermute | solution.py:622
  270.6 2.9 collective-permute-start.4
  279.1 12.4 %slice-start.11 = ((s8[4718592]{0:T(1024)(128)(4,1)}), s8[4194304]{0:T(1024)(128)(4,1)S(1)}, s32[]{:S(2)}) async-start(s8[4718592]{0:T(1024)(128)(4,1)} %bitcast.384), calls=%async_computation.11 | async-start | bytes 8388608 | tf_op jit(solution)/shard_map/cond
  282.8 8.7 %slice-start.12 = ((s8[4718592]{0:T(1024)(128)(4,1)}), s8[524288]{0:T(1024)(128)(4,1)S(1)}, s32[]{:S(2)}) async-start(s8[4718592]{0:T(1024)(128)(4,1)} %bitcast.384), calls=%async_computation.12 | async-start | bytes 1048576 | tf_op jit(solution)/shard_map/cond
  288.7 17.4 %slice-start.7 = ((s8[4718592]{0:T(1024)(128)(4,1)}), s8[4194304]{0:T(1024)(128)(4,1)S(1)}, s32[]{:S(2)}) async-start(s8[4718592]{0:T(1024)(128)(4,1)} %bitcast.364), calls=%async_computation.7 | async-start | bytes 8388608 | tf_op jit(solution)/shard_map/cond
  291.5 25.8 %copy-start.7 = (f32[4,228,768]{2,1,0:T(8,128)}, f32[4,228,768]{2,1,0:T(8,128)S(1)}, u32[]{:S(2)}) copy-start(f32[4,228,768]{2,1,0:T(8,128)S(1)} %get-tuple-element.415) | copy-start | bytes 8404996 | tf_op jit(solution)/shard_map/cond
  291.5 14.6 %slice-start.8 = ((s8[4718592]{0:T(1024)(128)(4,1)}), s8[524288]{0:T(1024)(128)(4,1)S(1)}, s32[]{:S(2)}) async-start(s8[4718592]{0:T(1024)(128)(4,1)} %bitcast.364), calls=%async_computation.8 | async-start | bytes 1048576 | tf_op jit(solution)/shard_map/cond
  344.4 13.6 %slice-start = ((s8[11403264]{0:T(1024)(128)(4,1)}), s8[4194304]{0:T(1024)(128)(4,1)S(1)}, s32[]{:S(2)}) async-start(s8[11403264]{0:T(1024)(128)(4,1)} %bitcast.318), calls=%async_computation | async-start | bytes 8388608 | tf_op jit(solution)/shard_map/cond
  344.4 13.6 %slice-start.1 = ((s8[11403264]{0:T(1024)(128)(4,1)}), s8[4194304]{0:T(1024)(128)(4,1)S(1)}, s32[]{:S(2)}) async-start(s8[11403264]{0:T(1024)(128)(4,1)} %bitcast.318), calls=%async_computation.1 | async-start | bytes 8388608 | tf_op jit(solution)/shard_map/cond
  344.4 13.6 %slice-start.2 = ((s8[11403264]{0:T(1024)(128)(4,1)}), s8[3014656]{0:T(1024)(128)(4,1)S(1)}, s32[]{:S(2)}) async-start(s8[11403264]{0:T(1024)(128)(4,1)} %bitcast.318), calls=%async_computation.2 | async-start | bytes 6029312 | tf_op jit(solution)/shard_map/cond
  358.0 7.5 %copy-start.15 = (bf16[4,228,768]{1,2,0:T(8,128)(2,1)S(1)}, bf16[4,228,768]{1,2,0:T(8,128)(2,1)}, u32[]{:S(2)}) copy-start(bf16[4,228,768]{1,2,0:T(8,128)(2,1)} %copy-done.14) | copy-start | bytes 4202500 | tf_op jit(solution)/shard_map/cond
  455.1 187.8 %copy-start.31 = (bf16[4,228,768]{2,0,1:T(4,128)(2,1)}, bf16[4,228,768]{2,0,1:T(4,128)(2,1)S(1)}, u32[]{:S(2)}) copy-start(bf16[4,228,768]{2,0,1:T(4,128)(2,1)S(1)} %get-tuple-element.372) | copy-start | bytes 4202500
  643.1 90.2 %collective-permute-start.3 = (bf16[4,228,384]{2,0,1:T(4,128)(2,1)S(1)}, bf16[4,228,384]{2,0,1:T(4,128)(2,1)}, u32[]{:S(2)}, u32[]{:S(2)}) collective-permute-start(bf16[4,228,384]{2,0,1:T(4,128)(2,1)S(1)} %constant_dynamic-slice_fusion.1), channel_id=1, source_target_pairs={{0,16},{16,0},{1,17},{17,1},{2,18},{18,2},{3,19},{19,3},{4,20},{20... | collective-permute-start | bytes 2101256 | tf_op jit(solution)/shard_map/ppermute | solution.py:622
  726.0 7.4 %copy-start.32 = (bf16[4,228,768]{2,0,1:T(4,128)(2,1)S(1)}, bf16[4,228,768]{2,0,1:T(4,128)(2,1)}, u32[]{:S(2)}) copy-start(bf16[4,228,768]{2,0,1:T(4,128)(2,1)} %copy-done.31) | copy-start | bytes 4202500
  (21 other events, 69.6 us)

commit v2 on v1

v2 whole, which is shorter than its diff:
```python
import functools

import jax
import jax.numpy as jnp
from jax import lax
from jax.experimental import pallas as pl
from jax.experimental.pallas import tpu as pltpu
from jax.sharding import PartitionSpec as P

PATCHES = 196
MESH = pl.DeviceIdType.MESH
bf16, f32 = jnp.bfloat16, jnp.float32
epsilon = 1e-06
far_below = -1000000000.0
HEAD = 64
SLAB = 128
TILE = 256
GELU_A = 0.7978845608028654
GELU_B = 0.044715


def nn(a, b):
    return jnp.dot(a, b, preferred_element_type=f32)


def nt(a, b):
    return lax.dot_general(a, b, (((1,), (1,)), ((), ())), preferred_element_type=f32)


def tn(a, b):
    return lax.dot_general(a, b, (((0,), (0,)), ((), ())), preferred_element_type=f32)


def normal(v):
    centered = v - jnp.mean(v, axis=-1, keepdims=True)
    spread = lax.rsqrt(jnp.mean(centered * centered, axis=-1, keepdims=True) + epsilon)
    return centered * spread, spread


def gelu_both(u):
    square = u * u
    bent = jnp.tanh(GELU_A * u * (1.0 + GELU_B * square))
    half = 0.5 * (1.0 + bent)
    slope = half + 0.5 * u * (1.0 - bent * bent) * (GELU_A * (1.0 + 3.0 * GELU_B * square))
    return u * half, slope


def at(start, size, unit):
    return pl.ds(pl.multiple_of(start, unit), size)


def fused_kernel(items, span, dec_len,
                 x_in, y_in, dz_in, wq_in, wo_in, wi_in, wd_in, wc_in, gain, shift, key_open, self_open,
                 panels, norms, dx_out, dec_out, dy_out,
                 w_qkv, w_out, w_up, w_down, w_cross,
                 qkv, prob, heads, low, rows_a, turned, hidden, result, active, slope, crossing, stage,
                 wsem, xsem, psem, send_sem, recv_sem):
    width = w_out.shape[0]
    hidden_units = w_up.shape[1]
    pairs = width // SLAB
    full = items * span
    blocks_up = hidden_units // width
    at_qkv, at_out, at_cross, at_up, at_down = 0, 3, 4, 6, 6 + blocks_up
    section = lax.axis_index("section")
    chip = lax.axis_index("batch")
    other = (1 - section, chip)

    barrier = pltpu.get_barrier_semaphore()
    pl.semaphore_signal(barrier, inc=1, device_id=other, device_id_type=MESH)

    weights = ((wq_in, w_qkv), (wo_in, w_out), (wi_in, w_up), (wd_in, w_down), (wc_in, w_cross))
    loads = [pltpu.make_async_copy(src, dst, wsem.at[n]) for n, (src, dst) in enumerate(weights)]

    lane = lax.broadcasted_iota(jnp.int32, (1, SLAB), 1)
    is_first = lane < HEAD
    mask_a = jnp.where(is_first, 1.0, 0.0).astype(bf16)
    mask_b = jnp.where(is_first, 0.0, 1.0).astype(bf16)
    scale = HEAD ** (-0.5)

    def stacked(slab, factor=1.0):
        return jnp.concatenate([slab * (mask_a * factor).astype(bf16), slab * (mask_b * factor).astype(bf16)], axis=0)

    def joined(both, rows):
        return jnp.where(is_first, both[:rows], both[rows:])

    def soft(scores, is_open):
        scores = jnp.where(is_open, scores, far_below)
        grown = jnp.exp(scores - jnp.max(scores, axis=-1, keepdims=True))
        return (grown * (1.0 / jnp.sum(grown, axis=-1, keepdims=True))).astype(bf16)

    def soft_back(p_low, dp):
        p = p_low.astype(f32)
        t = p * dp
        return (t - p * jnp.sum(t, axis=-1, keepdims=True)).astype(bf16)

    def wide(n):
        return at(n * width, width, width)

    def slab_of(n, h):
        return at(n * width + h * SLAB, SLAB, SLAB)

    def chunk(i):
        return pl.ds(i * span, span)

    def block_store(n, index):
        return pltpu.make_async_copy(stage.at[n % 2], panels.at[index], psem.at[n % 2])

    def emit(n, index, value):
        @pl.when(n >= 2)
        def _():
            block_store(n, index).wait()
        stage[n % 2] = value.astype(bf16)
        block_store(n, index).start()

    def norm_forward(value, index):
        unit, _ = normal(value)
        return (unit * gain[index : index + 1] + shift[index : index + 1]).astype(bf16)

    def norm_back(value, grad, index):
        unit, spread = normal(value)
        norms[index : index + 1] += jnp.sum(grad * unit, axis=0, keepdims=True)
        norms[3 + index : 4 + index] += jnp.sum(grad, axis=0, keepdims=True)
        scaled = grad * gain[index : index + 1]
        return spread * (
            scaled
            - jnp.mean(scaled, axis=-1, keepdims=True)
            - unit * jnp.mean(scaled * unit, axis=-1, keepdims=True)
        )

    def crossing_copy(source, n, tile):
        return pltpu.make_async_remote_copy(
            src_ref=source,
            dst_ref=crossing.at[:, at(tile * TILE, TILE, TILE)],
            send_sem=send_sem.at[n],
            recv_sem=recv_sem.at[tile],
            device_id=other,
            device_id_type=MESH,
        )

    tiles = width // TILE
    norms[...] = jnp.zeros_like(norms)

    @pl.when(section == 0)
    def _():
        x_load = pltpu.make_async_copy(x_in, low, xsem.at[0])
        x_load.start()
        for load in loads:
            load.start()
        x_load.wait()
        for i in range(items):
            rows_a[chunk(i)] = norm_forward(low[chunk(i)].astype(f32), 0)
        loads[0].wait()

        @pl.loop(0, 3)
        def _(j):
            for i in range(items):
                qkv[chunk(i), wide(j)] = nn(rows_a[chunk(i)], w_qkv[:, wide(j)]).astype(bf16)

        @pl.loop(0, items * pairs // 2)
        def _(it):
            i, h = it // (pairs // 2), 2 * (it % (pairs // 2))
            r = at(i * span, span, 16)
            for u in range(2):
                q, k, v = (qkv[r, slab_of(n, h + u)] for n in range(3))
                p = soft(nt(stacked(q, scale), k), key_open[i] > 0.0)
                prob[2 * it + u] = p
                heads[r, slab_of(0, h + u)] = joined(nn(p, v), span).astype(bf16)

        loads[1].wait()
        for i in range(items):
            r = chunk(i)
            value = low[r].astype(f32) + nn(heads[r], w_out[...])
            hidden[r] = value
            rows_a[r] = norm_forward(value, 1)
        loads[2].wait()

        @pl.loop(0, blocks_up)
        def _(j):
            for i in range(items):
                e, s = gelu_both(nn(rows_a[chunk(i)], w_up[:, wide(j)]))
                active[chunk(i), wide(j)] = e.astype(bf16)
                slope[chunk(i), wide(j)] = s.astype(bf16)

        loads[3].wait()
        for i in range(items):
            r = chunk(i)
            value = hidden[r] + nn(active[r], w_down[...])
            result[r] = value
            rows_a[r] = norm_forward(value, 2)
        loads[4].wait()
        pl.semaphore_wait(barrier, 1)

        def kv_send(n):
            return crossing_copy(turned.at[pl.ds(0, full), at((n % 3) * TILE, TILE, TILE)], n, n // 2 + tiles * (n % 2))

        for n in range(2 * tiles):
            tile = n // 2 + tiles * (n % 2)
            if n >= 3:
                kv_send(n - 3).wait_send()
            for i in range(items):
                turned[chunk(i), pl.ds((n % 3) * TILE, TILE)] = nn(rows_a[chunk(i)], w_cross[:, pl.ds(tile * TILE, TILE)]).astype(bf16)
            kv_send(n).start()
        for n in range(2 * tiles - 3, 2 * tiles):
            kv_send(n).wait_send()

        for n in range(2 * tiles):
            tile = n // 2 + tiles * (n % 2)
            crossing_copy(crossing.at[:, pl.ds(tile * TILE, TILE)], tile, tile).wait_recv()

        for i in range(items):
            r = chunk(i)
            value = norm_back(result[r], nt(crossing[r], w_cross[...]), 2)
            result[r] = value
            low[r] = value.astype(bf16)

        @pl.loop(0, 2)
        def _(j):
            emit(j, at_cross + j, tn(rows_a[...], crossing[:, wide(j)]))
        done = 2

        @pl.loop(0, blocks_up)
        def _(j):
            for i in range(items):
                r = chunk(i)
                slope[r, wide(j)] = (nt(low[r], w_down[wide(j)]) * slope[r, wide(j)].astype(f32)).astype(bf16)

        @pl.loop(0, blocks_up)
        def _(j):
            emit(done + j, at_down + j, tn(active[:, wide(j)], low[...]))
        done += blocks_up
        for i in range(items):
            rows_a[chunk(i)] = norm_forward(hidden[chunk(i)], 1)

        @pl.loop(0, blocks_up)
        def _(j):
            emit(done + j, at_up + j, tn(rows_a[...], slope[:, wide(j)]))
        done += blocks_up
        for i in range(items):
            r = chunk(i)
            value = result[r] + norm_back(hidden[r], nt(slope[r], w_up[...]), 1)
            result[r] = value
            low[r] = value.astype(bf16)
            rows_a[r] = nt(low[r], w_out[...]).astype(bf16)
        emit(done, at_out, tn(heads[...], low[...]))
        done += 1
        x_again = pltpu.make_async_copy(x_in, low, xsem.at[0])
        x_again.start()

        @pl.loop(0, items * pairs // 2)
        def _(it):
            i, h = it // (pairs // 2), 2 * (it % (pairs // 2))
            r = at(i * span, span, 16)
            for u in range(2):
                cq, ck, cv = (slab_of(n, h + u) for n in range(3))
                q, k, v = qkv[r, cq], qkv[r, ck], qkv[r, cv]
                both = stacked(rows_a[r, cq])
                p = prob[2 * it + u]
                ds = soft_back(p, nt(both, v))
                active[r, cq] = (joined(nn(ds, k), span) * scale).astype(bf16)
                active[r, ck] = tn(ds, stacked(q, scale)).astype(bf16)
                active[r, cv] = tn(p, both).astype(bf16)

        x_again.wait()
        for i in range(items):
            rows_a[chunk(i)] = norm_forward(low[chunk(i)].astype(f32), 0)

        @pl.loop(0, 3)
        def _(j):
            emit(done + j, at_qkv + j, tn(rows_a[...], active[:, wide(j)]))
        done += 3
        for i in range(items):
            r = chunk(i)
            grad = nt(active[r, pl.ds(0, 3 * width)], w_qkv[...])
            heads[r] = (result[r] + norm_back(low[r].astype(f32), grad, 0)).astype(bf16)
        dx_store = pltpu.make_async_copy(heads, dx_out, xsem.at[0])
        dx_store.start()
        block_store(0, 0).wait()
        block_store(1, 0).wait()
        dx_store.wait()

    @pl.when(section == 1)
    def _():
        dec = items * dec_len
        ra, rb, rc, rd = (pl.ds(n * dec, dec) for n in range(4))
        for n in (0, 1, 4, 2, 3):
            loads[n].start()
        rows_a[ra] = norm_forward(y_in[...].astype(f32), 0)
        loads[0].wait()

        @pl.loop(0, 3)
        def _(j):
            qkv[ra, wide(j)] = nn(rows_a[ra], w_qkv[:, wide(j)]).astype(bf16)

        own = self_open[...] > 0.0
        own = jnp.concatenate([own, own], axis=0)

        @pl.loop(0, pairs)
        def _(h):
            cq, ck, cv = (slab_of(n, h) for n in range(3))
            p = soft(nt(stacked(qkv[ra, cq], scale), qkv[ra, ck]), own)
            prob[h, pl.ds(0, 2 * dec), pl.ds(0, dec)] = p
            heads[ra, cq] = joined(nn(p, qkv[ra, cv]), dec).astype(bf16)

        loads[1].wait()
        value = y_in[...].astype(f32) + nn(heads[ra], w_out[...])
        hidden[ra] = value
        rows_a[rb] = norm_forward(value, 1)
        loads[4].wait()
        low[rb] = nn(rows_a[rb], w_cross[:, pl.ds(0, width)]).astype(bf16)
        loads[2].wait()
        loads[3].wait()

        part = 2 * dec_len
        spots = [(u, i) for u in range(TILE // SLAB) for i in range(items)]
        key_rows = jnp.concatenate([jnp.broadcast_to(key_open[i], (part, span)) for u, i in spots], axis=0)

        @pl.loop(0, tiles)
        def _(t):
            for tile in (t, tiles + t):
                crossing_copy(crossing.at[:, at(tile * TILE, TILE, TILE)], tile, tile).wait_recv()

            def slab(n, u):
                return at(n * width + t * TILE + u * SLAB, SLAB, SLAB)
            scores = [
                nt(stacked(low[pl.ds(dec + i * dec_len, dec_len), slab(0, u)], scale), crossing[chunk(i), slab(0, u)])
                for u, i in spots
            ]
            p = soft(jnp.concatenate(scores, axis=0), key_rows > 0.0)
            for u in range(TILE // SLAB):
                prob[pairs + t * (TILE // SLAB) + u, pl.ds(0, items * part)] = p[u * items * part : (u + 1) * items * part]
            for n, (u, i) in enumerate(spots):
                both = nn(p[n * part : (n + 1) * part], crossing[chunk(i), slab(1, u)])
                heads[pl.ds(dec + i * dec_len, dec_len), slab(0, u)] = joined(both, dec_len).astype(bf16)

        value = hidden[ra] + nn(heads[rb], w_cross[:, pl.ds(width, width)])
        hidden[rb] = value
        rows_a[rc] = norm_forward(value, 2)

        @pl.loop(0, blocks_up)
        def _(j):
            e, s = gelu_both(nn(rows_a[rc], w_up[:, wide(j)]))
            active[ra, wide(j)] = e.astype(bf16)
            active[rb, wide(j)] = (nt(dz_in[...], w_down[wide(j)]) * s).astype(bf16)

        value = dz_in[...].astype(f32) + norm_back(hidden[rb], nt(active[rb], w_up[...]), 2)
        result[ra] = value
        low[ra] = value.astype(bf16)
        rows_a[rd] = nt(low[ra], w_cross[:, pl.ds(width, width)]).astype(bf16)
        pl.semaphore_wait(barrier, 1)

        def kv_back(tile):
            return crossing_copy(slope.at[:, at(tile * TILE, TILE, TILE)], tile, tile)

        @pl.loop(0, tiles)
        def _(t):
            def slab(n, u):
                return at(n * width + t * TILE + u * SLAB, SLAB, SLAB)
            both = [stacked(rows_a[pl.ds(3 * dec + i * dec_len, dec_len), slab(0, u)]) for u, i in spots]
            dp = jnp.concatenate([nt(both[n], crossing[chunk(i), slab(1, u)]) for n, (u, i) in enumerate(spots)], axis=0)
            p = jnp.concatenate(
                [prob[pairs + t * (TILE // SLAB) + u, pl.ds(0, items * part)] for u in range(TILE // SLAB)], axis=0
            )
            ds = soft_back(p, dp)
            for n, (u, i) in enumerate(spots):
                lines = slice(n * part, (n + 1) * part)
                q = stacked(low[pl.ds(dec + i * dec_len, dec_len), slab(0, u)], scale)
                slope[chunk(i), slab(0, u)] = tn(ds[lines], q).astype(bf16)
                slope[chunk(i), slab(1, u)] = tn(p[lines], both[n]).astype(bf16)
            kv_back(t).start()
            kv_back(tiles + t).start()
            for n, (u, i) in enumerate(spots):
                lines = slice(n * part, (n + 1) * part)
                back = joined(nn(ds[lines], crossing[chunk(i), slab(0, u)]), dec_len) * scale
                low[pl.ds(3 * dec + i * dec_len, dec_len), slab(0, u)] = back.astype(bf16)

        @pl.loop(0, blocks_up)
        def _(j):
            emit(j, at_down + j, tn(active[ra, wide(j)], dz_in[...]))
        done = blocks_up

        @pl.loop(0, blocks_up)
        def _(j):
            emit(done + j, at_up + j, tn(rows_a[rc], active[rb, wide(j)]))
        done += blocks_up
        emit(done, at_cross + 1, tn(heads[rb], low[ra]))
        emit(done + 1, at_cross, tn(rows_a[rb], low[rd]))
        done += 2
        value = result[ra] + norm_back(hidden[ra], nt(low[rd], w_cross[:, pl.ds(0, width)]), 1)
        result[ra] = value
        low[ra] = value.astype(bf16)
        emit(done, at_out, tn(heads[ra], low[ra]))
        done += 1
        rows_a[rd] = nt(low[ra], w_out[...]).astype(bf16)

        @pl.loop(0, pairs)
        def _(h):
            cq, ck, cv = (slab_of(n, h) for n in range(3))
            q, k, v = qkv[ra, cq], qkv[ra, ck], qkv[ra, cv]
            both = stacked(rows_a[rd, cq])
            p = prob[h, pl.ds(0, 2 * dec), pl.ds(0, dec)]
            ds = soft_back(p, nt(both, v))
            qkv[rb, cq] = (joined(nn(ds, k), dec) * scale).astype(bf16)
            qkv[rb, ck] = tn(ds, stacked(q, scale)).astype(bf16)
            qkv[rb, cv] = tn(p, both).astype(bf16)

        @pl.loop(0, 3)
        def _(j):
            emit(done + j, at_qkv + j, tn(rows_a[ra], qkv[rb, wide(j)]))
        done += 3
        grad = nt(qkv[rb], w_qkv[...])
        dy_out[...] = (result[ra] + norm_back(y_in[...].astype(f32), grad, 0)).astype(bf16)
        dec_out[...] = (hidden[rb] + nn(active[ra], w_down[...])).astype(bf16)
        block_store(0, 0).wait()
        block_store(1, 0).wait()
        for tile in range(2 * tiles):
            kv_back(tile).wait_send()


def fused(x, y, dz, weights, gain, shift, key_open, self_open, items, span, dec_len, collective_id):
    wq, wo, wi, wd, wc = weights
    width, hidden_units = wi.shape
    full = items * span
    dec = items * dec_len
    count = sum(w.size for w in weights) // (width * width)
    here = pl.BlockSpec(memory_space=pltpu.VMEM)
    there = pl.BlockSpec(memory_space=pl.ANY)
    pairs = width // SLAB
    return pl.pallas_call(
        functools.partial(fused_kernel, items, span, dec_len),
        out_shape=(
            jax.ShapeDtypeStruct((count, width, width), bf16),
            jax.ShapeDtypeStruct((8, width), f32),
            jax.ShapeDtypeStruct((full, width), bf16),
            jax.ShapeDtypeStruct((dec, width), bf16),
            jax.ShapeDtypeStruct((dec, width), bf16),
        ),
        in_specs=[there, here, here] + [there] * 5 + [here] * 4,
        out_specs=(there, here, there, here, here),
        scratch_shapes=[
            pltpu.VMEM(wq.shape, bf16),
            pltpu.VMEM(wo.shape, bf16),
            pltpu.VMEM(wi.shape, bf16),
            pltpu.VMEM(wd.shape, bf16),
            pltpu.VMEM(wc.shape, bf16),
            pltpu.VMEM((full, 3 * width), bf16),
            pltpu.VMEM((items * pairs, 2 * span, span), bf16),
            pltpu.VMEM((full, width), bf16),
            pltpu.VMEM((full, width), bf16),
            pltpu.VMEM((full, width), bf16),
            pltpu.VMEM((full, width), bf16),
            pltpu.VMEM((full, width), f32),
            pltpu.VMEM((full, width), f32),
            pltpu.VMEM((full, hidden_units), bf16),
            pltpu.VMEM((full, hidden_units), bf16),
            pltpu.VMEM((full, 2 * width), bf16),
            pltpu.VMEM((2, width, width), bf16),
            pltpu.SemaphoreType.DMA((5,)),
            pltpu.SemaphoreType.DMA((1,)),
            pltpu.SemaphoreType.DMA((2,)),
            pltpu.SemaphoreType.DMA((2 * width // TILE,)),
            pltpu.SemaphoreType.DMA((2 * width // TILE,)),
        ],
        compiler_params=pltpu.CompilerParams(
            collective_id=collective_id, has_side_effects=True, vmem_limit_bytes=63 * 2**20
        ),
    )(x, y, dz, wq, wo, wi, wd, wc, gain, shift, key_open, self_open)


NZ = 4

def place():
    b = lax.axis_index("batch"); c = lax.axis_index("section")
    return b % 2, (b // 2) % 2, b // 4, c

def bid(x, y, z):
    return z * 4 + y * 2 + x

def ar_kernel(pairs, rows, width, across_block, g, norms, out, norms_out, acc, res, rx, up, dn, ry, nbuf, lsem, asend, arecv, zsend, zrecv, nsem):
    x, y, z, c = place()
    half, block, share = rows // 2, rows // 8, rows // 16

    def dev(x, y, z):
        return (c, bid(x, y, z))

    across = (dev(1 - x, y, z), dev(x, 1 - y, z))
    above, below = dev(x, y, z + 1), dev(x, y, z - 1)
    bit = (x, y)

    barrier = pltpu.get_barrier_semaphore()
    faraway = dev(x, y, (z + 2) % NZ)
    for d in across + (faraway,):
        pl.semaphore_signal(barrier, inc=1, device_id=d, device_id_type=MESH)

    @pl.when(z < NZ - 1)
    def _():
        pl.semaphore_signal(barrier, inc=1, device_id=above, device_id_type=MESH)

    @pl.when(z > 0)
    def _():
        pl.semaphore_signal(barrier, inc=1, device_id=below, device_id_type=MESH)

    pl.semaphore_wait(barrier, 3 + (z + NZ - 1) // NZ + (2 * NZ - 2 - z) // NZ)

    def rdma(src, dst, send, recv, device):
        return pltpu.make_async_remote_copy(src_ref=src, dst_ref=dst, send_sem=send, recv_sem=recv, device_id=device, device_id_type=MESH)

    def parts(t, f):
        p = 2 * t + f
        a, b = bit[f], bit[1 - f]
        own = a * half
        other = (1 - a) * half
        return p, own, other, b

    def rows_at(start, n):
        return pl.ds(pl.multiple_of(start, 16), n)

    def panel_of(array, p, start, n):
        columns = pl.ds(pl.multiple_of(p % across_block * width, 128), width)
        return array.at[p // across_block, rows_at(start, n), columns]

    def own_load(t, f):
        p, own, other, b = parts(t, f)
        return pltpu.make_async_copy(panel_of(g, p, own, half), acc.at[p], lsem.at[p, 0])

    def own_store(t, f, k):
        p, own, other, b = parts(t, f)
        start = own if k == 0 else other
        return pltpu.make_async_copy(res.at[p, rows_at(start, half)], panel_of(out, p, start, half), lsem.at[p, k + 1])

    def rs_a(t, f):
        p, own, other, b = parts(t, f)
        return rdma(panel_of(g, p, other, half), rx.at[p], asend.at[p, 0], arecv.at[p, 0], across[f])

    def rs_up(t, f, k):
        p, own, other, b = parts(t, f)
        return rdma(acc.at[p, pl.ds(k * block, block)], up.at[p, k], zsend.at[p, 0, k], zrecv.at[p, 0, k], above)

    def rs_dn(t, f, k):
        p, own, other, b = parts(t, f)
        return rdma(acc.at[p, pl.ds(k * block, block)], dn.at[p, k], zsend.at[p, 1, k], zrecv.at[p, 1, k], below)

    def rs_b(t, f):
        p, own, other, b = parts(t, f)
        return rdma(acc.at[p, rows_at(z * block + (1 - b) * share, share)], ry.at[p], asend.at[p, 1], arecv.at[p, 1], across[1 - f])

    def ag_b(t, f):
        p, own, other, b = parts(t, f)
        s = res.at[p, rows_at(own + z * block + b * share, share)]
        return rdma(s, s, asend.at[p, 2], arecv.at[p, 2], across[1 - f])

    def ag_up(t, f, k):
        p, own, other, b = parts(t, f)
        s = res.at[p, rows_at(own + k * block, block)]
        return rdma(s, s, zsend.at[p, 2, k], zrecv.at[p, 2, k], above)

    def ag_dn(t, f, k):
        p, own, other, b = parts(t, f)
        s = res.at[p, rows_at(own + k * block, block)]
        return rdma(s, s, zsend.at[p, 3, k], zrecv.at[p, 3, k], below)

    def ag_a(t, f):
        p, own, other, b = parts(t, f)
        s = res.at[p, rows_at(own, half)]
        return rdma(s, s, asend.at[p, 3], arecv.at[p, 3], across[f])

    def s0(t, f):
        rs_a(t, f).start()
        own_load(t, f).start()

    def s1(t, f):
        p, own, other, b = parts(t, f)
        own_load(t, f).wait()
        rs_a(t, f).wait()
        acc[p] = acc[p] + rx[p]

        @pl.when(z == 0)
        def _():
            for k in range(NZ - 1, 0, -1):
                rs_up(t, f, k).start()

        @pl.when(z == NZ - 1)
        def _():
            for k in range(NZ - 1):
                rs_dn(t, f, k).start()

    def chain(t, f, j):
        p, own, other, b = parts(t, f)

        @pl.when(z == j)
        def _():
            for k in range(NZ - 1, j - 1, -1):
                rs_up(t, f, k).wait_recv()
                r = pl.ds(k * block, block)
                acc[p, r] = acc[p, r] + up[p, k]
                if k > j:
                    rs_up(t, f, k).start()

        @pl.when(z == NZ - 1 - j)
        def _():
            for k in range(NZ - j):
                rs_dn(t, f, k).wait_recv()
                r = pl.ds(k * block, block)
                acc[p, r] = acc[p, r] + dn[p, k]
                if k < NZ - 1 - j:
                    rs_dn(t, f, k).start()

    def s4(t, f):
        chain(t, f, NZ - 1)
        rs_b(t, f).start()

    def s5(t, f):
        p, own, other, b = parts(t, f)
        rs_b(t, f).wait()
        mine = z * block + b * share
        res[p, rows_at(own + mine, share)] = acc[p, rows_at(mine, share)] + ry[p]
        ag_b(t, f).start()

    def s6(t, f):
        ag_b(t, f).wait()

        @pl.when(z < NZ - 1)
        def _():
            ag_up(t, f, z).start()

        @pl.when(z > 0)
        def _():
            ag_dn(t, f, z).start()

    def spread(t, f, j):
        @pl.when(z >= j)
        def _():
            ag_up(t, f, z - j).wait_recv()

            @pl.when(z < NZ - 1)
            def _():
                ag_up(t, f, z - j).start()

        @pl.when(z + j <= NZ - 1)
        def _():
            ag_dn(t, f, z + j).wait_recv()

            @pl.when(z > 0)
            def _():
                ag_dn(t, f, z + j).start()

    def s9(t, f):
        spread(t, f, NZ - 1)
        ag_a(t, f).start()
        own_store(t, f, 0).start()

    def s10(t, f):
        ag_a(t, f).wait()
        own_store(t, f, 1).start()
        for k in range(NZ):
            @pl.when((z < k))
            def _(k=k):
                rs_up(t, f, k).wait_send()

            @pl.when((z > k))
            def _(k=k):
                rs_dn(t, f, k).wait_send()

            @pl.when((k <= z) & (z < NZ - 1))
            def _(k=k):
                ag_up(t, f, k).wait_send()

            @pl.when((k >= z) & (z > 0))
            def _(k=k):
                ag_dn(t, f, k).wait_send()

    def s11(t, f):
        own_store(t, f, 0).wait()
        own_store(t, f, 1).wait()

    mates = across + (dev(x, y, z + 1 - 2 * (z % 2)), faraway)

    def norm_swap(j):
        return rdma(norms_out, nbuf.at[j], nsem.at[0, j], nsem.at[1, j], mates[j])

    norms_out[...] = norms[...]
    norm_swap(0).start()

    stages = [s0, s1] + [functools.partial(lambda j, t, f: chain(t, f, j), j) for j in range(1, NZ - 1)] + [s4, s5, s6] + [
        functools.partial(lambda j, t, f: spread(t, f, j), j) for j in range(1, NZ - 1)] + [s9, s10, s11]
    ahead = 2

    def tick(tau, carry):
        for j in range(4):

            @pl.when(tau == 3 * j + 3)
            def _(j=j):
                norm_swap(j).wait()
                norms_out[...] = norms_out[...] + nbuf[j]
                if j < 3:
                    norm_swap(j + 1).start()

        for i, stage in enumerate(stages):
            lag = 0 if i == 0 else i - 1 + ahead
            t = tau - lag

            @pl.when((t >= 0) & (t < pairs))
            def _(stage=stage, t=t):
                stage(t, 0)
                stage(t, 1)
        return carry
    lax.fori_loop(0, pairs + len(stages) - 2 + ahead, tick, 0)


def all_reduce(g, norms, collective_id):
    blocks, rows, block_width = g.shape
    width = 256
    across_block = block_width // width
    n = blocks * across_block
    half, block, share = rows // 2, rows // 8, rows // 16
    bf = jnp.bfloat16
    return pl.pallas_call(
        functools.partial(ar_kernel, n // 2, rows, width, across_block),
        out_shape=(jax.ShapeDtypeStruct(g.shape, bf), jax.ShapeDtypeStruct(norms.shape, norms.dtype)),
        in_specs=[pl.BlockSpec(memory_space=pl.ANY), pl.BlockSpec(memory_space=pltpu.VMEM)],
        out_specs=(pl.BlockSpec(memory_space=pl.ANY), pl.BlockSpec(memory_space=pltpu.VMEM)),
        scratch_shapes=[
            pltpu.VMEM((n, half, width), bf),
            pltpu.VMEM((n, rows, width), bf),
            pltpu.VMEM((n, half, width), bf),
            pltpu.VMEM((n, NZ, block, width), bf),
            pltpu.VMEM((n, NZ, block, width), bf),
            pltpu.VMEM((n, share, width), bf),
            pltpu.VMEM((4,) + norms.shape, norms.dtype),
            pltpu.SemaphoreType.DMA((n, 3)),
            pltpu.SemaphoreType.DMA((n, 4)),
            pltpu.SemaphoreType.DMA((n, 4)),
            pltpu.SemaphoreType.DMA((n, 4, NZ)),
            pltpu.SemaphoreType.DMA((n, 4, NZ)),
            pltpu.SemaphoreType.DMA((2, 4)),
        ],
        compiler_params=pltpu.CompilerParams(collective_id=collective_id, has_side_effects=True, vmem_limit_bytes=60 * 2**20),
    )(g, norms)


def unpack_kernel(counts, panels, *outs):
    step = pl.program_id(0)
    first = 0
    for count, out in zip(counts, outs):

        @pl.when((step >= first) & (step < first + count))
        def _(out=out):
            out[0] = panels[0].astype(f32)

        first += count


def unpack(panels, shapes):
    total, high, wide = panels.shape
    counts = [rows * columns // (high * wide) for rows, columns in shapes]
    out_specs = []
    first = 0
    for (rows, columns), count in zip(shapes, counts):
        across = columns // wide

        def place_of(step, first=first, count=count, across=across):
            own = jnp.clip(step - first, 0, count - 1)
            return 0, own // across, own % across

        out_specs.append(pl.BlockSpec((1, high, wide), place_of))
        first += count
    return pl.pallas_call(
        functools.partial(unpack_kernel, counts),
        grid=(total,),
        out_shape=[jax.ShapeDtypeStruct((1,) + shape, f32) for shape in shapes],
        in_specs=[pl.BlockSpec((1, high, wide), lambda step: (step, 0, 0))],
        out_specs=out_specs,
        compiler_params=pltpu.CompilerParams(vmem_limit_bytes=48 * 2**20),
    )(panels)


def per_device(
    enc_input,
    dec_input,
    out_grad,
    attn_qkv,
    attn_out,
    mlp_in,
    mlp_out,
    cross_proj,
    norm_gain,
    norm_shift,
    image_count,
    prefix_len,
    suffix_len,
):
    section = lax.axis_index("section")
    items, enc_len, width = enc_input.shape
    dec_len = dec_input.shape[1]
    span = -(-enc_len // 16) * 16
    weights = (attn_qkv[0], attn_out[0], mlp_in[0], mlp_out[0], cross_proj[0])
    positions = jnp.arange(span, dtype=jnp.int32)[None, :]
    has_image = (jnp.arange(items, dtype=jnp.int32) < image_count[0])[:, None]
    key_open = jnp.where(positions < PATCHES, has_image, positions - PATCHES < prefix_len[:, None])
    key_open = (key_open & (positions < enc_len)).astype(f32)[:, None, :]
    places = jnp.arange(items * dec_len, dtype=jnp.int32)
    item, spot = places // dec_len, places % dec_len
    self_open = (
        (item[:, None] == item[None, :])
        & (spot[None, :] <= spot[:, None])
        & (spot[None, :] < jnp.repeat(suffix_len, dec_len)[None, :])
    ).astype(f32)
    x = jnp.pad(enc_input, ((0, 0), (0, span - enc_len), (0, 0))).reshape(items * span, width)
    panels, norms, dx, dec_out, dy = fused(
        x,
        dec_input.reshape(-1, width),
        out_grad.reshape(-1, width),
        weights,
        norm_gain[0].astype(f32),
        norm_shift[0].astype(f32),
        key_open,
        self_open,
        items,
        span,
        dec_len,
        1,
    )
    if lax.axis_size("batch") == 16:
        panels, norms = all_reduce(panels, norms, 0)
    else:
        panels, norms = lax.psum(panels, "batch"), lax.psum(norms, "batch")
    dx, dec_out, dy, panels = lax.optimization_barrier((dx, dec_out, dy, panels))
    order = (0, 1, 4, 2, 3)
    blocks = unpack(panels, [weights[n].shape for n in order])
    grads = [blocks[order.index(n)] for n in range(len(order))]
    half = width // 2
    on_first = section == 0
    own_start, other_start = section * half, (1 - section) * half

    def columns(array, start):
        return lax.dynamic_slice_in_dim(array, start, half, 2)

    def swapped(array):
        return lax.ppermute(columns(array, other_start), "section", [(0, 1), (1, 0)])

    dx = dx.reshape(items, span, width)[:, :enc_len]
    dec_out = dec_out.reshape(dec_input.shape)
    dy = dy.reshape(dec_input.shape)
    return (
        jnp.where(on_first, swapped(dec_out), columns(dec_out, own_start)),
        jnp.where(on_first, columns(dx, own_start), swapped(dx)),
        jnp.where(on_first, swapped(dy), columns(dy, own_start)),
        *grads,
        norms[None, :3],
        norms[None, 3:6],
    )


def solution(mesh):
    items = P("batch", None, None)
    matrix = P("section", None, None)
    halves = P("batch", None, "section")
    return jax.shard_map(
        per_device,
        mesh=mesh,
        in_specs=(items,) * 3 + (matrix,) * 7 + (P("batch"),) * 3,
        out_specs=(halves,) * 3 + (matrix,) * 7,
        check_vma=False,
    )
```

time: 742 us -> 370 us (0.50)
  Pallas kernels: 149 us -> 350 us
  local copies, waits for them, and re-layouts: 198 us -> 5.35 us
  starting transfers between devices: 158 us -> 0.97 us
  matrix products: 145 us -> 0 us
  other arithmetic: 72.8 us -> 5.36 us
    pallas_call x1 -> x3, Pallas kernels: 149 us -> 350 us  [the longest x1 202 us: all_reduce(): pl.pallas_call(functools.partial(ar_kernel, n // 2, rows, width, across_b...]
    ppermute x5 -> x3, starting transfers between devices: 158 us -> 0.97 us  [swapped(): lax.ppermute(columns(array, other_start), 'section', [(0, 1), (1, 0)])]
    dot_general x22 -> x0, matrix products: 145 us -> none  [the longest x5 38.2 us: backward_product(): jnp.einsum('blf,df->bld', grad_rows, matrix, preferred_element_type=jnp.f...]
    convert_element_type x8 -> x0, local copies, waits for them, and re-layouts: 53.6 us -> none  [the longest x6 46.8 us: from_panels(): return split.transpose(0, 2, 1, 3).reshape(shape).astype(jnp.float32)]
    cond x76 -> x0, local copies, waits for them, and re-layouts: 47.3 us -> none  [the longest x2 23.3 us: per_device(): lax.cond(section == 0, encode_back, lambda: (blank(encode_back)[0], dec_p...]
    unnamed x19 -> x14, local copies, waits for them, and re-layouts: 37.6 us -> 3.03 us
    convert_element_type x10 -> x3, other arithmetic: 33.1 us -> 2.73 us  [the longest x1 1.33 us: per_device(): norm_shift[0].astype(f32)]
    reduce_sum x12 -> x0, other arithmetic: 24.3 us -> none  [the longest x4 8.52 us: layer_norm(): variance = jnp.mean(centered * centered, axis=-1, keepdims=True)]
  transfers between devices with their start and end apart: 5 -> 3, of which waited for: 2 -> 0; matrix products, arithmetic and copies ran while one was open for 13% -> 1% of each run, Pallas kernels for 0% -> 6%
where the time goes in v2:
time: 370 us; the launch traced here: 364 us
  Pallas kernels  350 us (95%)
  other arithmetic  5.36 us (1%)
  local copies, waits for them, and re-layouts  5.35 us (1%)
    pallas_call x1, Pallas kernels, all_reduce(): pl.pallas_call(functools.partial(ar_kernel, n // 2, rows, width, across_b...  202 us
    pallas_call x1, Pallas kernels, fused(): pl.pallas_call(functools.partial(fused_kernel, items, span, dec_len), out...  128 us
    pallas_call x1, Pallas kernels, unpack(): pl.pallas_call(functools.partial(unpack_kernel, counts), grid=(total,), o...  20.8 us
  transfers between devices with their start and end apart: 3, of which 0 were waited for; matrix products, arithmetic and copies ran while one was open for 1% of the time, Pallas kernels for 6%

profile of v2, /device:TPU:0, one launch (start us, length us, event | category | flops | bytes accessed | tf_op | source)
XLA Modules:
  0.0 363.7 jit_solution(8691098608233930076)
XLA Ops:
  1.4 0.7 broadcast_in_dim.36
  2.1 0.1 broadcast_in_dim_reshape.3
  2.2 1.5 copy.30
  3.7 1.3 bitcast_convert_fusion
  5.0 1.2 pad.4.clone
  6.2 0.7 and_convert_fusion.self_open
  7.0 0.7 and_convert_fusion.1.key_open
  7.6 127.7 %shard_map.204 = (bf16[14,768,768]{2,1,0:T(8,128)(2,1)}, f32[8,768]{1,0:T(8,128)}, bf16[960,768]{1,0:T(8,128)(2,1)}, bf16[128,768]{1,0:T(8,128)(2,1)}, bf16[128,768]{1,0:T(8,128)(2,1)}) custom-call(bf16[960,768]{1,0:T(8,128)(2,1)} %bitcast.23, bf16[128,768]{1,0:T(8,128)(2,1)} %bitcast.30, bf16[128,768]{1,0:T(8,128)(2,1)} %bitcast.31, ...), custom_call_target="tpu_custom_call" | custom-call | tf_op jit(solution)/shard_map/pallas_call | solution.py:428
  135.3 201.9 %shard_map.205 = (bf16[14,768,768]{2,1,0:T(8,128)(2,1)}, f32[8,768]{1,0:T(8,128)}) custom-call(bf16[14,768,768]{2,1,0:T(8,128)(2,1)} %get-tuple-element.29.g, f32[8,768]{1,0:T(8,128)} %get-tuple-element.30.norms), custom_call_target="tpu_custom_call" | custom-call | tf_op jit(solution)/shard_map/pallas_call | solution.py:716
  337.3 0.1 collective-permute-start.2
  337.4 0.1 slice.12
  337.5 0.2 constant_dynamic-slice_fusion.2
  337.6 0.3 copy.29
  337.9 0.6 collective-permute-start.1
  338.5 0.3 collective-permute-start
  338.9 0.6 copy.26
  339.5 0.6 copy.25
  340.1 20.8 %shard_map.206 = (f32[1,768,2304]{2,1,0:T(8,128)}, f32[1,768,768]{2,1,0:T(8,128)}, f32[1,768,1536]{2,1,0:T(8,128)}, f32[1,768,3072]{2,1,0:T(8,128)}, f32[1,3072,768]{2,1,0:T(8,128)}) custom-call(bf16[14,768,768]{2,1,0:T(8,128)(2,1)} %get-tuple-element.35.panels), custom_call_target="tpu_custom_call" | custom-call | tf_op jit(solution)/shard_map/pallas_call | solution.py:766
  360.8 0.0 collective-permute-done.2
  360.9 0.7 dynamic-slice_select_fusion
  361.5 0.0 collective-permute-done
  361.5 0.7 dynamic-slice_select_fusion.1
  362.2 0.0 collective-permute-done.1
  362.2 1.3 copy_select_fusion
  (18 shorter events, 0.1 us)
Async XLA Ops:
  0.6 6.3 %copy-start.4 = (s32[4]{0:T(128)S(1)}, s32[4]{0:T(128)}, u32[]{:S(2)}) copy-start(s32[4]{0:T(128)} %param.24) | copy-start | bytes 52
  135.3 201.9 %copy-start.2 = (bf16[128,768]{1,0:T(8,128)(2,1)S(1)}, bf16[128,768]{1,0:T(8,128)(2,1)}, u32[]{:S(2)}) copy-start(bf16[128,768]{1,0:T(8,128)(2,1)} %get-tuple-element.34) | copy-start | bytes 589828
  135.3 202.0 %copy-start = (bf16[960,768]{1,0:T(8,128)(2,1)S(1)}, bf16[960,768]{1,0:T(8,128)(2,1)}, u32[]{:S(2)}) copy-start(bf16[960,768]{1,0:T(8,128)(2,1)} %get-tuple-element.33) | copy-start | bytes 4423684
  337.3 23.6 %collective-permute-start.2 = (bf16[4,32,384]{2,1,0:T(8,128)(2,1)S(1)}, bf16[4,32,384]{2,1,0:T(8,128)(2,1)S(1)}, u32[]{:S(2)}, u32[]{:S(2)}) collective-permute-start(bf16[4,32,384]{2,1,0:T(8,128)(2,1)S(1)} %constant_dynamic-slice_fusion), channel_id=1, source_target_pairs={{0,16},{16,0},{1,17},{17,1},{2,18},{18,2},{3,19},{19,3},{4,20},{20... | collective-permute-start | bytes 294920 | tf_op jit(solution)/shard_map/ppermute | solution.py:838
  337.4 1.1 copy-start.1
  337.4 1.5 copy-start.3
  337.9 24.3 %collective-permute-start.1 = (bf16[4,228,384]{2,0,1:T(4,128)(2,1)S(1)}, bf16[4,228,384]{2,0,1:T(4,128)(2,1)S(1)}, u32[]{:S(2)}, u32[]{:S(2)}) collective-permute-start(bf16[4,228,384]{2,0,1:T(4,128)(2,1)S(1)} %copy.29), channel_id=1, source_target_pairs={{0,16},{16,0},{1,17},{17,1},{2,18},{18,2},{3,19},{19,3},{4,20},{20... | collective-permute-start | bytes 2101256 | tf_op jit(solution)/shard_map/ppermute | solution.py:838
  338.5 23.0 %collective-permute-start = (bf16[4,32,384]{2,1,0:T(8,128)(2,1)S(1)}, bf16[4,32,384]{2,1,0:T(8,128)(2,1)S(1)}, u32[]{:S(2)}, u32[]{:S(2)}) collective-permute-start(bf16[4,32,384]{2,1,0:T(8,128)(2,1)S(1)} %constant_dynamic-slice_fusion.3), channel_id=1, source_target_pairs={{0,16},{16,0},{1,17},{17,1},{2,18},{18,2},{3,19},{19,3},{4,20},{20... | collective-permute-start | bytes 294920 | tf_op jit(solution)/shard_map/ppermute | solution.py:838

commit v3 on v2

--- a/solution.py
+++ b/solution.py
@@ -19,6 +19,18 @@
 GELU_B = 0.044715
 
 
+NZ = 4
+
+
+def place():
+    b = lax.axis_index("batch")
+    return b % 2, (b // 2) % 2, b // 4, lax.axis_index("section")
+
+
+def bid(x, y, z):
+    return z * 4 + y * 2 + x
+
+
 def nn(a, b):
     return jnp.dot(a, b, preferred_element_type=f32)
 
@@ -49,24 +61,121 @@
     return pl.ds(pl.multiple_of(start, unit), size)
 
 
-def fused_kernel(items, span, dec_len,
+def fused_kernel(items, span, dec_len, gathers,
                  x_in, y_in, dz_in, wq_in, wo_in, wi_in, wd_in, wc_in, gain, shift, key_open, self_open,
-                 panels, norms, dx_out, dec_out, dy_out,
+                 panels, norms, dx_out, dec_out, dy_out, pool,
                  w_qkv, w_out, w_up, w_down, w_cross,
                  qkv, prob, heads, low, rows_a, turned, hidden, result, active, slope, crossing, stage,
-                 wsem, xsem, psem, send_sem, recv_sem):
+                 wsem, xsem, psem, send_sem, recv_sem, zsend, zrecv, asend, arecv, lsem, hsend, hrecv):
     width = w_out.shape[0]
     hidden_units = w_up.shape[1]
     pairs = width // SLAB
     full = items * span
     blocks_up = hidden_units // width
-    at_qkv, at_out, at_cross, at_up, at_down = 0, 3, 4, 6, 6 + blocks_up
+    at_qkv, at_out, at_cross, at_up, at_down = 0, 3, 4, 6, 7
     section = lax.axis_index("section")
     chip = lax.axis_index("batch")
     other = (1 - section, chip)
 
     barrier = pltpu.get_barrier_semaphore()
     pl.semaphore_signal(barrier, inc=1, device_id=other, device_id_type=MESH)
+    x, y, z, _ = place()
+    beside = ((section, bid(1 - x, y, z)), (section, bid(x, 1 - y, z)))
+    above, below = (section, bid(x, y, z + 1)), (section, bid(x, y, z - 1))
+    if gathers:
+
+        @pl.when(section == 1)
+        def _():
+            for device in beside:
+                pl.semaphore_signal(barrier, inc=1, device_id=device, device_id_type=MESH)
+
+            @pl.when(z < NZ - 1)
+            def _():
+                pl.semaphore_signal(barrier, inc=1, device_id=above, device_id_type=MESH)
+
+            @pl.when(z > 0)
+            def _():
+                pl.semaphore_signal(barrier, inc=1, device_id=below, device_id_type=MESH)
+
+    def pool_copy(kind, half, src, dst, send, recv, device):
+        return pltpu.make_async_remote_copy(
+            src_ref=src, dst_ref=dst, send_sem=send, recv_sem=recv, device_id=device, device_id_type=MESH
+        )
+
+    def half_rows(half):
+        size = items * dec_len // 2
+        return pl.ds(half * size, size)
+
+    def along_z(kind, half, way, k, source=None):
+        spot = pool.at[kind, k, y, x, half_rows(half)]
+        return pool_copy(
+            kind, half, spot if source is None else source, spot,
+            zsend.at[kind, half, way, k], zrecv.at[kind, half, way, k], (above, below)[way],
+        )
+
+    def along_a(kind, half):
+        spot = pool.at[kind, :, y, x, half_rows(half)]
+        return pool_copy(kind, half, spot, spot, asend.at[kind, half, 0], arecv.at[kind, half, 0], beside[half])
+
+    def along_b(kind, half):
+        spot = pool.at[kind, :, y, :, half_rows(half)] if half == 0 else pool.at[kind, :, :, x, half_rows(half)]
+        return pool_copy(kind, half, spot, spot, asend.at[kind, half, 1], arecv.at[kind, half, 1], beside[1 - half])
+
+    def own_copy(kind, source):
+        return pltpu.make_async_copy(source, pool.at[kind, z, y, x], lsem.at[kind])
+
+    def gather_step(kind, step, source):
+        if not gathers:
+            return
+        if step == 0:
+            own_copy(kind, source).start()
+        for half in range(2):
+            if step == 0:
+                mine = source.at[half_rows(half)]
+
+                @pl.when(z < NZ - 1)
+                def _():
+                    along_z(kind, half, 0, z, mine).start()
+
+                @pl.when(z > 0)
+                def _():
+                    along_z(kind, half, 1, z, mine).start()
+            elif step < NZ:
+
+                @pl.when(z >= step)
+                def _():
+                    along_z(kind, half, 0, z - step).wait_recv()
+
+                    @pl.when(z < NZ - 1)
+                    def _():
+                        along_z(kind, half, 0, z - step).start()
+
+                @pl.when(z + step <= NZ - 1)
+                def _():
+                    along_z(kind, half, 1, z + step).wait_recv()
+
+                    @pl.when(z > 0)
+                    def _():
+                        along_z(kind, half, 1, z + step).start()
+            elif step == NZ:
+                if half == 0:
+                    own_copy(kind, source).wait()
+                along_a(kind, half).start()
+            elif step == NZ + 1:
+                along_a(kind, half).wait_recv()
+                along_b(kind, half).start()
+            else:
+                along_b(kind, half).wait()
+                along_a(kind, half).wait_send()
+                for k in range(NZ):
+
+                    @pl.when((k <= z) & (z < NZ - 1))
+                    def _(k=k):
+                        along_z(kind, half, 0, k).wait_send()
+
+                    @pl.when((k >= z) & (z > 0))
+                    def _(k=k):
+                        along_z(kind, half, 1, k).wait_send()
 
     weights = ((wq_in, w_qkv), (wo_in, w_out), (wi_in, w_up), (wd_in, w_down), (wc_in, w_cross))
     loads = [pltpu.make_async_copy(src, dst, wsem.at[n]) for n, (src, dst) in enumerate(weights)]
@@ -137,6 +246,17 @@
             device_id_type=MESH,
         )
 
+    def end_copy(n):
+        dec = items * dec_len
+        return pltpu.make_async_remote_copy(
+            src_ref=heads.at[pl.ds((2 + n) * dec, dec), pl.ds(0, width // 2)],
+            dst_ref=(dy_out, dec_out)[n],
+            send_sem=hsend.at[n],
+            recv_sem=hrecv.at[n],
+            device_id=other,
+            device_id_type=MESH,
+        )
+
     tiles = width // TILE
     norms[...] = jnp.zeros_like(norms)
 
@@ -226,14 +346,14 @@
 
         @pl.loop(0, blocks_up)
         def _(j):
-            emit(done + j, at_down + j, tn(active[:, wide(j)], low[...]))
+            emit(done + j, at_down + 2 * j, tn(active[:, wide(j)], low[...]))
         done += blocks_up
         for i in range(items):
             rows_a[chunk(i)] = norm_forward(hidden[chunk(i)], 1)
 
         @pl.loop(0, blocks_up)
         def _(j):
-            emit(done + j, at_up + j, tn(rows_a[...], slope[:, wide(j)]))
+            emit(done + j, at_up + 2 * j, tn(rows_a[...], slope[:, wide(j)]))
         done += blocks_up
         for i in range(items):
             r = chunk(i)
@@ -277,6 +397,8 @@
         block_store(0, 0).wait()
         block_store(1, 0).wait()
         dx_store.wait()
+        for n in range(2):
+            end_copy(n).wait_recv()
 
     @pl.when(section == 1)
     def _():
@@ -285,6 +407,9 @@
         for n in (0, 1, 4, 2, 3):
             loads[n].start()
         rows_a[ra] = norm_forward(y_in[...].astype(f32), 0)
+        if gathers:
+            pl.semaphore_wait(barrier, 3 + (z + NZ - 1) // NZ + (2 * NZ - 2 - z) // NZ)
+        gather_step(0, 0, dz_in)
         loads[0].wait()
 
         @pl.loop(0, 3)
@@ -301,6 +426,7 @@
             prob[h, pl.ds(0, 2 * dec), pl.ds(0, dec)] = p
             heads[ra, cq] = joined(nn(p, qkv[ra, cv]), dec).astype(bf16)
 
+        gather_step(0, 1, dz_in)
         loads[1].wait()
         value = y_in[...].astype(f32) + nn(heads[ra], w_out[...])
         hidden[ra] = value
@@ -309,6 +435,8 @@
         low[rb] = nn(rows_a[rb], w_cross[:, pl.ds(0, width)]).astype(bf16)
         loads[2].wait()
         loads[3].wait()
+        for step in range(2, NZ + 3):
+            gather_step(0, step, dz_in)
 
         part = 2 * dec_len
         spots = [(u, i) for u in range(TILE // SLAB) for i in range(items)]
@@ -335,6 +463,8 @@
         value = hidden[ra] + nn(heads[rb], w_cross[:, pl.ds(width, width)])
         hidden[rb] = value
         rows_a[rc] = norm_forward(value, 2)
+        mid = rows_a.at[rc]
+        gather_step(1, 0, mid)
 
         @pl.loop(0, blocks_up)
         def _(j):
@@ -342,11 +472,14 @@
             active[ra, wide(j)] = e.astype(bf16)
             active[rb, wide(j)] = (nt(dz_in[...], w_down[wide(j)]) * s).astype(bf16)
 
+        gather_step(1, 1, mid)
+
         value = dz_in[...].astype(f32) + norm_back(hidden[rb], nt(active[rb], w_up[...]), 2)
         result[ra] = value
         low[ra] = value.astype(bf16)
         rows_a[rd] = nt(low[ra], w_cross[:, pl.ds(width, width)]).astype(bf16)
-        pl.semaphore_wait(barrier, 1)
+        if not gathers:
+            pl.semaphore_wait(barrier, 1)
 
         def kv_back(tile):
             return crossing_copy(slope.at[:, at(tile * TILE, TILE, TILE)], tile, tile)
@@ -373,24 +506,30 @@
                 back = joined(nn(ds[lines], crossing[chunk(i), slab(0, u)]), dec_len) * scale
                 low[pl.ds(3 * dec + i * dec_len, dec_len), slab(0, u)] = back.astype(bf16)
 
-        @pl.loop(0, blocks_up)
-        def _(j):
-            emit(j, at_down + j, tn(active[ra, wide(j)], dz_in[...]))
-        done = blocks_up
-
-        @pl.loop(0, blocks_up)
-        def _(j):
-            emit(done + j, at_up + j, tn(rows_a[rc], active[rb, wide(j)]))
-        done += blocks_up
+        gather_step(1, 2, mid)
+
+        done = 0
+        if not gathers:
+
+            @pl.loop(0, blocks_up)
+            def _(j):
+                emit(j, at_down + 2 * j, tn(active[ra, wide(j)], dz_in[...]))
+
+            @pl.loop(0, blocks_up)
+            def _(j):
+                emit(blocks_up + j, at_up + 2 * j, tn(rows_a[rc], active[rb, wide(j)]))
+            done = 2 * blocks_up
         emit(done, at_cross + 1, tn(heads[rb], low[ra]))
         emit(done + 1, at_cross, tn(rows_a[rb], low[rd]))
         done += 2
+        gather_step(1, 3, mid)
         value = result[ra] + norm_back(hidden[ra], nt(low[rd], w_cross[:, pl.ds(0, width)]), 1)
         result[ra] = value
         low[ra] = value.astype(bf16)
         emit(done, at_out, tn(heads[ra], low[ra]))
         done += 1
         rows_a[rd] = nt(low[ra], w_out[...]).astype(bf16)
+        gather_step(1, 4, mid)
 
         @pl.loop(0, pairs)
         def _(h):
@@ -403,20 +542,32 @@
             qkv[rb, ck] = tn(ds, stacked(q, scale)).astype(bf16)
             qkv[rb, cv] = tn(p, both).astype(bf16)
 
+        gather_step(1, 5, mid)
+
         @pl.loop(0, 3)
         def _(j):
             emit(done + j, at_qkv + j, tn(rows_a[ra], qkv[rb, wide(j)]))
         done += 3
         grad = nt(qkv[rb], w_qkv[...])
-        dy_out[...] = (result[ra] + norm_back(y_in[...].astype(f32), grad, 0)).astype(bf16)
-        dec_out[...] = (hidden[rb] + nn(active[ra], w_down[...])).astype(bf16)
+        half_width = width // 2
+        ends = (
+            (result[ra] + norm_back(y_in[...].astype(f32), grad, 0)).astype(bf16),
+            (hidden[rb] + nn(active[ra], w_down[...])).astype(bf16),
+        )
+        for n, (value, out) in enumerate(zip(ends, (dy_out, dec_out))):
+            out[...] = value[:, half_width:]
+            heads[pl.ds((2 + n) * dec, dec), pl.ds(0, half_width)] = value[:, :half_width]
+            end_copy(n).start()
         block_store(0, 0).wait()
         block_store(1, 0).wait()
+        for n in range(2):
+            end_copy(n).wait_send()
         for tile in range(2 * tiles):
             kv_back(tile).wait_send()
-
-
-def fused(x, y, dz, weights, gain, shift, key_open, self_open, items, span, dec_len, collective_id):
+        gather_step(1, 6, mid)
+
+
+def fused(x, y, dz, weights, gain, shift, key_open, self_open, items, span, dec_len, gathers, collective_id):
     wq, wo, wi, wd, wc = weights
     width, hidden_units = wi.shape
     full = items * span
@@ -426,16 +577,17 @@
     there = pl.BlockSpec(memory_space=pl.ANY)
     pairs = width // SLAB
     return pl.pallas_call(
-        functools.partial(fused_kernel, items, span, dec_len),
+        functools.partial(fused_kernel, items, span, dec_len, gathers),
         out_shape=(
             jax.ShapeDtypeStruct((count, width, width), bf16),
             jax.ShapeDtypeStruct((8, width), f32),
             jax.ShapeDtypeStruct((full, width), bf16),
-            jax.ShapeDtypeStruct((dec, width), bf16),
-            jax.ShapeDtypeStruct((dec, width), bf16),
+            jax.ShapeDtypeStruct((dec, width // 2), bf16),
+            jax.ShapeDtypeStruct((dec, width // 2), bf16),
+            jax.ShapeDtypeStruct((2, NZ, 2, 2, dec, width), bf16),
         ),
         in_specs=[there, here, here] + [there] * 5 + [here] * 4,
-        out_specs=(there, here, there, here, here),
+        out_specs=(there, here, there, here, here, there),
         scratch_shapes=[
             pltpu.VMEM(wq.shape, bf16),
             pltpu.VMEM(wo.shape, bf16),
@@ -459,6 +611,13 @@
             pltpu.SemaphoreType.DMA((2,)),
             pltpu.SemaphoreType.DMA((2 * width // TILE,)),
             pltpu.SemaphoreType.DMA((2 * width // TILE,)),
+            pltpu.SemaphoreType.DMA((2, 2, 2, NZ)),
+            pltpu.SemaphoreType.DMA((2, 2, 2, NZ)),
+            pltpu.SemaphoreType.DMA((2, 2, 2)),
+            pltpu.SemaphoreType.DMA((2, 2, 2)),
+            pltpu.SemaphoreType.DMA((2,)),
+            pltpu.SemaphoreType.DMA((2,)),
+            pltpu.SemaphoreType.DMA((2,)),
         ],
         compiler_params=pltpu.CompilerParams(
             collective_id=collective_id, has_side_effects=True, vmem_limit_bytes=63 * 2**20
@@ -466,17 +625,9 @@
     )(x, y, dz, wq, wo, wi, wd, wc, gain, shift, key_open, self_open)
 
 
-NZ = 4
-
-def place():
-    b = lax.axis_index("batch"); c = lax.axis_index("section")
-    return b % 2, (b // 2) % 2, b // 4, c
-
-def bid(x, y, z):
-    return z * 4 + y * 2 + x
-
-def ar_kernel(pairs, rows, width, across_block, g, norms, out, norms_out, acc, res, rx, up, dn, ry, nbuf, lsem, asend, arecv, zsend, zrecv, nsem):
+def ar_kernel(pairs, rows, width, across_block, g, norms, dx, out, norms_out, dx_half, acc, res, rx, up, dn, ry, nbuf, lsem, asend, arecv, zsend, zrecv, nsem, dsem):
     x, y, z, c = place()
+    pairs = pairs[0] + (pairs[1] - pairs[0]) * c
     half, block, share = rows // 2, rows // 8, rows // 16
 
     def dev(x, y, z):
@@ -499,10 +650,25 @@
     def _():
         pl.semaphore_signal(barrier, inc=1, device_id=below, device_id_type=MESH)
 
-    pl.semaphore_wait(barrier, 3 + (z + NZ - 1) // NZ + (2 * NZ - 2 - z) // NZ)
+    mate = (1 - c, bid(x, y, z))
+
+    @pl.when(c == 1)
+    def _():
+        pl.semaphore_signal(barrier, inc=1, device_id=mate, device_id_type=MESH)
+
+    pl.semaphore_wait(barrier, 4 - c + (z + NZ - 1) // NZ + (2 * NZ - 2 - z) // NZ)
 
     def rdma(src, dst, send, recv, device):
         return pltpu.make_async_remote_copy(src_ref=src, dst_ref=dst, send_sem=send, recv_sem=recv, device_id=device, device_id_type=MESH)
+
+    half_width = dx.shape[1] // 2
+    dx_own = pltpu.make_async_copy(dx.at[:, pl.ds(0, half_width)], dx_half, dsem.at[0])
+    dx_other = rdma(dx.at[:, pl.ds(half_width, half_width)], dx_half, dsem.at[1], dsem.at[2], mate)
+
+    @pl.when(c == 0)
+    def _():
+        dx_own.start()
+        dx_other.start()
 
     def parts(t, f):
         p = 2 * t + f
@@ -705,8 +871,17 @@
         return carry
     lax.fori_loop(0, pairs + len(stages) - 2 + ahead, tick, 0)
 
-
-def all_reduce(g, norms, collective_id):
+    @pl.when(c == 0)
+    def _():
+        dx_own.wait()
+        dx_other.wait_send()
+
+    @pl.when(c == 1)
+    def _():
+        dx_other.wait_recv()
+
+
+def all_reduce(g, norms, dx, counts, collective_id):
     blocks, rows, block_width = g.shape
     width = 256
     across_block = block_width // width
@@ -714,10 +889,14 @@
     half, block, share = rows // 2, rows // 8, rows // 16
     bf = jnp.bfloat16
     return pl.pallas_call(
-        functools.partial(ar_kernel, n // 2, rows, width, across_block),
-        out_shape=(jax.ShapeDtypeStruct(g.shape, bf), jax.ShapeDtypeStruct(norms.shape, norms.dtype)),
-        in_specs=[pl.BlockSpec(memory_space=pl.ANY), pl.BlockSpec(memory_space=pltpu.VMEM)],
-        out_specs=(pl.BlockSpec(memory_space=pl.ANY), pl.BlockSpec(memory_space=pltpu.VMEM)),
+        functools.partial(ar_kernel, [count * across_block // 2 for count in counts], rows, width, across_block),
+        out_shape=(
+            jax.ShapeDtypeStruct(g.shape, bf),
+            jax.ShapeDtypeStruct(norms.shape, norms.dtype),
+            jax.ShapeDtypeStruct((dx.shape[0], dx.shape[1] // 2), bf),
+        ),
+        in_specs=[pl.BlockSpec(memory_space=pl.ANY), pl.BlockSpec(memory_space=pltpu.VMEM), pl.BlockSpec(memory_space=pl.ANY)],
+        out_specs=(pl.BlockSpec(memory_space=pl.ANY), pl.BlockSpec(memory_space=pltpu.VMEM), pl.BlockSpec(memory_space=pl.ANY)),
         scratch_shapes=[
             pltpu.VMEM((n, half, width), bf),
             pltpu.VMEM((n, rows, width), bf),
@@ -732,45 +911,108 @@
             pltpu.SemaphoreType.DMA((n, 4, NZ)),
             pltpu.SemaphoreType.DMA((n, 4, NZ)),
             pltpu.SemaphoreType.DMA((2, 4)),
+            pltpu.SemaphoreType.DMA((3,)),
         ],
         compiler_params=pltpu.CompilerParams(collective_id=collective_id, has_side_effects=True, vmem_limit_bytes=60 * 2**20),
-    )(g, norms)
-
-
-def unpack_kernel(counts, panels, *outs):
+    )(g, norms, dx)
+
+
+def finish_kernel(counts, gathers, panels, pool, up_in, down_in, *rest):
+    outs, (rows, grads, w_up, w_down, active, bent, sems) = rest[:5], rest[5:]
     step = pl.program_id(0)
+    section = lax.axis_index("section")
+    plain = counts[0] + counts[1] + counts[2]
     first = 0
-    for count, out in zip(counts, outs):
+    for count, out in zip(counts[:3], outs):
 
         @pl.when((step >= first) & (step < first + count))
         def _(out=out):
             out[0] = panels[0].astype(f32)
 
         first += count
-
-
-def unpack(panels, shapes):
+    up, down = outs[3:]
+    turn = (step - plain) % 2
+    if gathers:
+        width = rows.shape[1]
+        loads = [
+            pltpu.make_async_copy(src, dst, sems.at[n])
+            for n, (src, dst) in enumerate(
+                ((pool.at[1], rows), (pool.at[0], grads), (up_in, w_up), (down_in, w_down))
+            )
+        ]
+
+        @pl.when((step == 0) & (section == 1))
+        def _():
+            for load in loads:
+                load.start()
+
+        @pl.when((step == plain) & (section == 1))
+        def _():
+            for load in loads:
+                load.wait()
+
+        @pl.when((step >= plain) & (turn == 0) & (section == 1))
+        def _():
+            cols = at((step - plain) // 2 * width, width, width)
+            size = 512
+
+            @pl.loop(0, rows.shape[0] // size)
+            def _(i):
+                r = at(i * size, size, size)
+                e, s = gelu_both(nn(rows[r], w_up[:, cols]))
+                active[r] = e.astype(bf16)
+                bent[r] = (nt(grads[r], w_down[cols]) * s).astype(bf16)
+            up[0] = tn(rows[...], bent[...])
+
+        @pl.when((step >= plain) & (turn == 1) & (section == 1))
+        def _():
+            down[0] = tn(active[...], grads[...])
+
+    summed = (section == 0) if gathers else (section >= 0)
+
+    @pl.when((step >= plain) & (turn == 0) & summed)
+    def _():
+        up[0] = panels[0].astype(f32)
+
+    @pl.when((step >= plain) & (turn == 1) & summed)
+    def _():
+        down[0] = panels[0].astype(f32)
+
+
+def finish(panels, pool, w_up, w_down, shapes, gathers):
     total, high, wide = panels.shape
     counts = [rows * columns // (high * wide) for rows, columns in shapes]
+    plain = sum(counts[:3])
     out_specs = []
     first = 0
-    for (rows, columns), count in zip(shapes, counts):
-        across = columns // wide
-
-        def place_of(step, first=first, count=count, across=across):
-            own = jnp.clip(step - first, 0, count - 1)
-            return 0, own // across, own % across
+    for (rows, columns), count in zip(shapes[:3], counts):
+
+        def place_of(step, first=first, count=count):
+            return 0, 0, jnp.clip(step - first, 0, count - 1)
 
         out_specs.append(pl.BlockSpec((1, high, wide), place_of))
         first += count
+    out_specs.append(pl.BlockSpec((1, high, wide), lambda step: (0, 0, jnp.clip((step - plain) // 2, 0, counts[3] - 1))))
+    out_specs.append(pl.BlockSpec((1, high, wide), lambda step: (0, jnp.clip((step - plain - 1) // 2, 0, counts[4] - 1), 0)))
+    there = pl.BlockSpec(memory_space=pl.ANY)
+    gathered = pool.shape[1] if gathers else 16
     return pl.pallas_call(
-        functools.partial(unpack_kernel, counts),
+        functools.partial(finish_kernel, counts, gathers),
         grid=(total,),
         out_shape=[jax.ShapeDtypeStruct((1,) + shape, f32) for shape in shapes],
-        in_specs=[pl.BlockSpec((1, high, wide), lambda step: (step, 0, 0))],
+        in_specs=[pl.BlockSpec((1, high, wide), lambda step: (step, 0, 0)), there, there, there],
         out_specs=out_specs,
-        compiler_params=pltpu.CompilerParams(vmem_limit_bytes=48 * 2**20),
-    )(panels)
+        scratch_shapes=[
+            pltpu.VMEM((gathered, wide), bf16),
+            pltpu.VMEM((gathered, wide), bf16),
+            pltpu.VMEM(w_up.shape, bf16),
+            pltpu.VMEM(w_down.shape, bf16),
+            pltpu.VMEM((gathered, wide), bf16),
+            pltpu.VMEM((gathered, wide), bf16),
+            pltpu.SemaphoreType.DMA((4,)),
+        ],
+        compiler_params=pltpu.CompilerParams(vmem_limit_bytes=63 * 2**20),
+    )(panels, pool, w_up, w_down)
 
 
 def per_device(
@@ -805,7 +1047,8 @@
         & (spot[None, :] < jnp.repeat(suffix_len, dec_len)[None, :])
     ).astype(f32)
     x = jnp.pad(enc_input, ((0, 0), (0, span - enc_len), (0, 0))).reshape(items * span, width)
-    panels, norms, dx, dec_out, dy = fused(
+    gathers = lax.axis_size("batch") == 16
+    panels, norms, dx, dec_out, dy, pool = fused(
         x,
         dec_input.reshape(-1, width),
         out_grad.reshape(-1, width),
@@ -817,33 +1060,27 @@
         items,
         span,
         dec_len,
+        gathers,
         1,
     )
-    if lax.axis_size("batch") == 16:
-        panels, norms = all_reduce(panels, norms, 0)
+    if gathers:
+        blocks = panels.shape[0]
+        panels, norms, dx_half = all_reduce(panels, norms, dx, (blocks, blocks - 2 * mlp_in.shape[2] // width), 0)
     else:
         panels, norms = lax.psum(panels, "batch"), lax.psum(norms, "batch")
-    dx, dec_out, dy, panels = lax.optimization_barrier((dx, dec_out, dy, panels))
+        half = width // 2
+        theirs = lax.dynamic_slice_in_dim(dx, (1 - section) * half, half, 1)
+        theirs = lax.ppermute(theirs, "section", [(0, 1), (1, 0)])
+        dx_half = jnp.where(section == 0, dx[:, :half], theirs)
     order = (0, 1, 4, 2, 3)
-    blocks = unpack(panels, [weights[n].shape for n in order])
+    pool = pool.reshape(2, -1, width) if gathers else pool[:, 0, 0, 0]
+    blocks = finish(panels, pool, weights[2], weights[3], [weights[n].shape for n in order], gathers)
     grads = [blocks[order.index(n)] for n in range(len(order))]
     half = width // 2
-    on_first = section == 0
-    own_start, other_start = section * half, (1 - section) * half
-
-    def columns(array, start):
-        return lax.dynamic_slice_in_dim(array, start, half, 2)
-
-    def swapped(array):
-        return lax.ppermute(columns(array, other_start), "section", [(0, 1), (1, 0)])
-
-    dx = dx.reshape(items, span, width)[:, :enc_len]
-    dec_out = dec_out.reshape(dec_input.shape)
-    dy = dy.reshape(dec_input.shape)
     return (
-        jnp.where(on_first, swapped(dec_out), columns(dec_out, own_start)),
-        jnp.where(on_first, columns(dx, own_start), swapped(dx)),
-        jnp.where(on_first, swapped(dy), columns(dy, own_start)),
+        dec_out.reshape(items, dec_len, half),
+        dx_half.reshape(items, span, half)[:, :enc_len],
+        dy.reshape(items, dec_len, half),
         *grads,
         norms[None, :3],
         norms[None, 3:6],

time: 370 us -> 332 us (0.90)
  Pallas kernels: 350 us -> 311 us
  local copies, waits for them, and re-layouts: 5.35 us -> 9.17 us
    pallas_call x3, Pallas kernels: 350 us -> 311 us  [the longest x1 159 us: all_reduce(): pl.pallas_call(functools.partial(ar_kernel, [count * across_block // 2 fo...]
  transfers between devices with their start and end apart: 3 -> 0, of which waited for: 0 -> 0; matrix products, arithmetic and copies ran while one was open for 1% -> 0% of each run, Pallas kernels for 6% -> 0%
where the time goes in v3:
time: 332 us; the launch traced here: 325 us
  Pallas kernels  311 us (94%)
  local copies, waits for them, and re-layouts  9.17 us (3%)
  other arithmetic  3.4 us (1%)
    pallas_call x1, Pallas kernels, all_reduce(): pl.pallas_call(functools.partial(ar_kernel, [count * across_block // 2 fo...  159 us
    pallas_call x1, Pallas kernels, fused(): pl.pallas_call(functools.partial(fused_kernel, items, span, dec_len, gath...  132 us
    pallas_call x1, Pallas kernels, finish(): pl.pallas_call(functools.partial(finish_kernel, counts, gathers), grid=(t...  20.5 us

profile of v3, /device:TPU:0, one launch (start us, length us, event | category | flops | bytes accessed | tf_op | source)
XLA Modules:
  0.0 325.4 jit_solution(15957379353961190372)
XLA Ops:
  1.3 1.3 and_convert_fusion.1.key_open
  2.7 0.7 broadcast_in_dim.36
  3.4 0.1 broadcast_in_dim_reshape.3
  3.5 1.3 bitcast_convert_fusion
  4.8 0.7 and_convert_fusion.self_open
  5.5 1.5 copy.28
  7.1 1.2 pad.4.clone
  8.3 131.6 %shard_map.204 = (bf16[14,768,768]{2,1,0:T(8,128)(2,1)}, f32[8,768]{1,0:T(8,128)}, bf16[960,768]{1,0:T(8,128)(2,1)}, bf16[128,384]{1,0:T(8,128)(2,1)}, bf16[128,...) custom-call(bf16[960,768]{1,0:T(8,128)(2,1)} %bitcast.29, bf16[128,768]{1,0:T(8,128)(2,1)} %bitcast.34, ...), custom_call_target="tpu_custom_call" | custom-call | tf_op jit(solution)/shard_map/pallas_call | solution.py:579
  139.9 158.8 %shard_map.205 = (bf16[14,768,768]{2,1,0:T(8,128)(2,1)}, f32[8,768]{1,0:T(8,128)}, bf16[960,384]{1,0:T(8,128)(2,1)}) custom-call(bf16[14,768,768]{2,1,0:T(8,128)(2,1)} %get-tuple-element.25.g, f32[8,768]{1,0:T(8,128)} %get-tuple-element.26.norms, bf16[960,768]{1,0:T(8,128)(2,1)} %get-tuple-element.27.dx), custom_call_target="tpu_custom_call" | custom-call | tf_op jit(solution)/shard_map/pallas_call | solution.py:891
  298.7 1.2 slice.12
  299.9 1.1 copy.27
  301.0 0.8 slice_bitcast_fusion
  301.8 0.6 copy.26
  302.4 0.6 copy.25
  303.1 0.0 copy-start.1
  303.1 0.0 copy-start
  303.1 20.5 %shard_map.206 = (f32[1,768,2304]{2,1,0:T(8,128)}, f32[1,768,768]{2,1,0:T(8,128)}, f32[1,768,1536]{2,1,0:T(8,128)}, f32[1,768,3072]{2,1,0:T(8,128)}, f32[1,3072,768]{2,1,0:T(8,128)}) custom-call(bf16[14,768,768]{2,1,0:T(8,128)(2,1)} %get-tuple-element.30.panels, bf16[2,2048,768]{2,1,0:T(8,128)(2,1)} %bitcast.28, bf16[768,3072]{1,0:T(8,128)(2,1)} %bitcast.25, ...), custom_call_target="tpu_custom_call" | custom-call | tf_op jit(solution)/shard_map/pallas_call | solution.py:999
  323.6 0.0 copy-done.1
  323.6 0.6 copy.32
  324.3 0.0 copy-done
  324.3 0.6 copy.33
  (5 shorter events, 0.0 us)
Async XLA Ops:
  303.1 20.6 %copy-start.1 = (bf16[128,384]{1,0:T(8,128)(2,1)S(1)}, bf16[128,384]{1,0:T(8,128)(2,1)}, u32[]{:S(2)}) copy-start(bf16[128,384]{1,0:T(8,128)(2,1)} %get-tuple-element.24) | copy-start | bytes 294916
  303.1 21.2 %copy-start = (bf16[128,384]{1,0:T(8,128)(2,1)S(1)}, bf16[128,384]{1,0:T(8,128)(2,1)}, u32[]{:S(2)}) copy-start(bf16[128,384]{1,0:T(8,128)(2,1)} %get-tuple-element.29) | copy-start | bytes 294916

commit v4 on v3

--- a/solution.py
+++ b/solution.py
@@ -625,10 +625,14 @@
     )(x, y, dz, wq, wo, wi, wd, wc, gain, shift, key_open, self_open)
 
 
+AHEAD = 2
+LATE = 2
+
+
 def ar_kernel(pairs, rows, width, across_block, g, norms, dx, out, norms_out, dx_half, acc, res, rx, up, dn, ry, nbuf, lsem, asend, arecv, zsend, zrecv, nsem, dsem):
     x, y, z, c = place()
     pairs = pairs[0] + (pairs[1] - pairs[0]) * c
-    half, block, share = rows // 2, rows // 8, rows // 16
+    half, block = rows // 2, rows // 8
 
     def dev(x, y, z):
         return (c, bid(x, y, z))
@@ -691,43 +695,40 @@
     def own_store(t, f, k):
         p, own, other, b = parts(t, f)
         start = own if k == 0 else other
-        return pltpu.make_async_copy(res.at[p, rows_at(start, half)], panel_of(out, p, start, half), lsem.at[p, k + 1])
+        return pltpu.make_async_copy(res.at[p, rows_at(start, half)], panel_of(out, p, start, half), lsem.at[p, k])
 
     def rs_a(t, f):
         p, own, other, b = parts(t, f)
-        return rdma(panel_of(g, p, other, half), rx.at[p], asend.at[p, 0], arecv.at[p, 0], across[f])
-
-    def rs_up(t, f, k):
+        return rdma(panel_of(g, p, other, half), rx.at[p], asend.at[p], arecv.at[p, 0], across[f])
+
+    def rs_up(t, f, j):
+        p = 2 * t + f
+        r = pl.ds((j + 1) * block, (NZ - 1 - j) * block)
+        return rdma(acc.at[p, r], up.at[p, r], zsend.at[p, 0], zrecv.at[p, 0, 0], above)
+
+    def rs_dn(t, f, j):
+        p = 2 * t + f
+        r = pl.ds(0, j * block)
+        return rdma(acc.at[p, r], dn.at[p, r], zsend.at[p, 1], zrecv.at[p, 1, 0], below)
+
+    def both_b(t, f):
         p, own, other, b = parts(t, f)
-        return rdma(acc.at[p, pl.ds(k * block, block)], up.at[p, k], zsend.at[p, 0, k], zrecv.at[p, 0, k], above)
-
-    def rs_dn(t, f, k):
+        return rdma(acc.at[p, rows_at(z * block, block)], ry.at[p], asend.at[p], arecv.at[p, 1], across[1 - f])
+
+    def ag_up(t, f, m):
         p, own, other, b = parts(t, f)
-        return rdma(acc.at[p, pl.ds(k * block, block)], dn.at[p, k], zsend.at[p, 1, k], zrecv.at[p, 1, k], below)
-
-    def rs_b(t, f):
+        s = res.at[p, rows_at(own + (z - m) * block, block)]
+        return rdma(s, s, zsend.at[p, 0], zrecv.at[p, 0, 1 + m], above)
+
+    def ag_dn(t, f, m):
         p, own, other, b = parts(t, f)
-        return rdma(acc.at[p, rows_at(z * block + (1 - b) * share, share)], ry.at[p], asend.at[p, 1], arecv.at[p, 1], across[1 - f])
-
-    def ag_b(t, f):
-        p, own, other, b = parts(t, f)
-        s = res.at[p, rows_at(own + z * block + b * share, share)]
-        return rdma(s, s, asend.at[p, 2], arecv.at[p, 2], across[1 - f])
-
-    def ag_up(t, f, k):
-        p, own, other, b = parts(t, f)
-        s = res.at[p, rows_at(own + k * block, block)]
-        return rdma(s, s, zsend.at[p, 2, k], zrecv.at[p, 2, k], above)
-
-    def ag_dn(t, f, k):
-        p, own, other, b = parts(t, f)
-        s = res.at[p, rows_at(own + k * block, block)]
-        return rdma(s, s, zsend.at[p, 3, k], zrecv.at[p, 3, k], below)
+        s = res.at[p, rows_at(own + (z + m) * block, block)]
+        return rdma(s, s, zsend.at[p, 1], zrecv.at[p, 1, 1 + m], below)
 
     def ag_a(t, f):
         p, own, other, b = parts(t, f)
         s = res.at[p, rows_at(own, half)]
-        return rdma(s, s, asend.at[p, 3], arecv.at[p, 3], across[f])
+        return rdma(s, s, asend.at[p], arecv.at[p, 2], across[f])
 
     def s0(t, f):
         rs_a(t, f).start()
@@ -741,73 +742,69 @@
 
         @pl.when(z == 0)
         def _():
-            for k in range(NZ - 1, 0, -1):
-                rs_up(t, f, k).start()
+            rs_up(t, f, 0).start()
 
         @pl.when(z == NZ - 1)
         def _():
-            for k in range(NZ - 1):
-                rs_dn(t, f, k).start()
+            rs_dn(t, f, NZ - 1).start()
 
     def chain(t, f, j):
-        p, own, other, b = parts(t, f)
+        p = 2 * t + f
 
         @pl.when(z == j)
         def _():
-            for k in range(NZ - 1, j - 1, -1):
-                rs_up(t, f, k).wait_recv()
-                r = pl.ds(k * block, block)
-                acc[p, r] = acc[p, r] + up[p, k]
-                if k > j:
-                    rs_up(t, f, k).start()
+            rs_up(t, f, j - 1).wait_recv()
+            r = pl.ds(j * block, (NZ - j) * block)
+            acc[p, r] = acc[p, r] + up[p, r]
+            if j < NZ - 1:
+                rs_up(t, f, j).start()
 
         @pl.when(z == NZ - 1 - j)
         def _():
-            for k in range(NZ - j):
-                rs_dn(t, f, k).wait_recv()
-                r = pl.ds(k * block, block)
-                acc[p, r] = acc[p, r] + dn[p, k]
-                if k < NZ - 1 - j:
-                    rs_dn(t, f, k).start()
+            rs_dn(t, f, NZ - j).wait_recv()
+            r = pl.ds(0, (NZ - j) * block)
+            acc[p, r] = acc[p, r] + dn[p, r]
+            if j < NZ - 1:
+                rs_dn(t, f, NZ - 1 - j).start()
 
     def s4(t, f):
         chain(t, f, NZ - 1)
-        rs_b(t, f).start()
+        both_b(t, f).start()
 
     def s5(t, f):
         p, own, other, b = parts(t, f)
-        rs_b(t, f).wait()
-        mine = z * block + b * share
-        res[p, rows_at(own + mine, share)] = acc[p, rows_at(mine, share)] + ry[p]
-        ag_b(t, f).start()
-
-    def s6(t, f):
-        ag_b(t, f).wait()
-
-        @pl.when(z < NZ - 1)
-        def _():
-            ag_up(t, f, z).start()
-
-        @pl.when(z > 0)
-        def _():
-            ag_dn(t, f, z).start()
+        both_b(t, f).wait()
+        res[p, rows_at(own + z * block, block)] = acc[p, rows_at(z * block, block)] + ry[p]
+
+        for j in range(NZ):
+
+            @pl.when(z == j)
+            def _(j=j):
+                if j < NZ - 1:
+                    rs_up(t, f, j).wait_send()
+                    ag_up(t, f, 0).start()
+                if j > 0:
+                    rs_dn(t, f, j).wait_send()
+                    ag_dn(t, f, 0).start()
 
     def spread(t, f, j):
         @pl.when(z >= j)
         def _():
-            ag_up(t, f, z - j).wait_recv()
+            ag_up(t, f, j - 1).wait_recv()
 
             @pl.when(z < NZ - 1)
             def _():
-                ag_up(t, f, z - j).start()
+                ag_up(t, f, j - 1).wait_send()
+                ag_up(t, f, j).start()
 
         @pl.when(z + j <= NZ - 1)
         def _():
-            ag_dn(t, f, z + j).wait_recv()
+            ag_dn(t, f, j - 1).wait_recv()
 
             @pl.when(z > 0)
             def _():
-                ag_dn(t, f, z + j).start()
+                ag_dn(t, f, j - 1).wait_send()
+                ag_dn(t, f, j).start()
 
     def s9(t, f):
         spread(t, f, NZ - 1)
@@ -817,22 +814,13 @@
     def s10(t, f):
         ag_a(t, f).wait()
         own_store(t, f, 1).start()
-        for k in range(NZ):
-            @pl.when((z < k))
-            def _(k=k):
-                rs_up(t, f, k).wait_send()
-
-            @pl.when((z > k))
-            def _(k=k):
-                rs_dn(t, f, k).wait_send()
-
-            @pl.when((k <= z) & (z < NZ - 1))
-            def _(k=k):
-                ag_up(t, f, k).wait_send()
-
-            @pl.when((k >= z) & (z > 0))
-            def _(k=k):
-                ag_dn(t, f, k).wait_send()
+        @pl.when(z < NZ - 1)
+        def _():
+            ag_up(t, f, 0).wait_send()
+
+        @pl.when(z > 0)
+        def _():
+            ag_dn(t, f, 0).wait_send()
 
     def s11(t, f):
         own_store(t, f, 0).wait()
@@ -846,9 +834,13 @@
     norms_out[...] = norms[...]
     norm_swap(0).start()
 
-    stages = [s0, s1] + [functools.partial(lambda j, t, f: chain(t, f, j), j) for j in range(1, NZ - 1)] + [s4, s5, s6] + [
-        functools.partial(lambda j, t, f: spread(t, f, j), j) for j in range(1, NZ - 1)] + [s9, s10, s11]
-    ahead = 2
+    stages = (
+        [(0, s0), (AHEAD, s1)]
+        + [(AHEAD + j, functools.partial(lambda j, t, f: chain(t, f, j), j)) for j in range(1, NZ - 1)]
+        + [(AHEAD + NZ - 1, s4), (AHEAD + NZ, s5)]
+        + [(AHEAD + NZ + j, functools.partial(lambda j, t, f: spread(t, f, j), j)) for j in range(1, NZ - 1)]
+        + [(AHEAD + 2 * NZ - 1, s9), (AHEAD + 2 * NZ + LATE, s10), (AHEAD + 2 * NZ + 1 + LATE, s11)]
+    )
 
     def tick(tau, carry):
         for j in range(4):
@@ -860,8 +852,7 @@
                 if j < 3:
                     norm_swap(j + 1).start()
 
-        for i, stage in enumerate(stages):
-            lag = 0 if i == 0 else i - 1 + ahead
+        for lag, stage in stages:
             t = tau - lag
 
             @pl.when((t >= 0) & (t < pairs))
@@ -869,7 +860,7 @@
                 stage(t, 0)
                 stage(t, 1)
         return carry
-    lax.fori_loop(0, pairs + len(stages) - 2 + ahead, tick, 0)
+    lax.fori_loop(0, pairs + AHEAD + 2 * NZ + 2 + LATE, tick, 0)
 
     @pl.when(c == 0)
     def _():
@@ -886,7 +877,7 @@
     width = 256
     across_block = block_width // width
     n = blocks * across_block
-    half, block, share = rows // 2, rows // 8, rows // 16
+    half, block = rows // 2, rows // 8
     bf = jnp.bfloat16
     return pl.pallas_call(
         functools.partial(ar_kernel, [count * across_block // 2 for count in counts], rows, width, across_block),
@@ -901,15 +892,15 @@
             pltpu.VMEM((n, half, width), bf),
             pltpu.VMEM((n, rows, width), bf),
             pltpu.VMEM((n, half, width), bf),
-            pltpu.VMEM((n, NZ, block, width), bf),
-            pltpu.VMEM((n, NZ, block, width), bf),
-            pltpu.VMEM((n, share, width), bf),
+            pltpu.VMEM((n, half, width), bf),
+            pltpu.VMEM((n, half, width), bf),
+            pltpu.VMEM((n, block, width), bf),
             pltpu.VMEM((4,) + norms.shape, norms.dtype),
+            pltpu.SemaphoreType.DMA((n, 2)),
+            pltpu.SemaphoreType.DMA((n,)),
             pltpu.SemaphoreType.DMA((n, 3)),
-            pltpu.SemaphoreType.DMA((n, 4)),
-            pltpu.SemaphoreType.DMA((n, 4)),
-            pltpu.SemaphoreType.DMA((n, 4, NZ)),
-            pltpu.SemaphoreType.DMA((n, 4, NZ)),
+            pltpu.SemaphoreType.DMA((n, 2)),
+            pltpu.SemaphoreType.DMA((n, 2, NZ)),
             pltpu.SemaphoreType.DMA((2, 4)),
             pltpu.SemaphoreType.DMA((3,)),
         ],
@@ -917,92 +908,102 @@
     )(g, norms, dx)
 
 
+SLOTS = 4
+
+
 def finish_kernel(counts, gathers, panels, pool, up_in, down_in, *rest):
-    outs, (rows, grads, w_up, w_down, active, bent, sems) = rest[:5], rest[5:]
-    step = pl.program_id(0)
+    outs = rest[:5]
+    inbox, stage, rows, grads, w_up, w_down, active, bent, sems, in_sems, out_sems = rest[5:]
+    width = panels.shape[1]
+    plain = sum(counts[:3])
+    total = sum(counts)
     section = lax.axis_index("section")
-    plain = counts[0] + counts[1] + counts[2]
-    first = 0
+    targets = []
     for count, out in zip(counts[:3], outs):
-
-        @pl.when((step >= first) & (step < first + count))
-        def _(out=out):
-            out[0] = panels[0].astype(f32)
-
-        first += count
-    up, down = outs[3:]
-    turn = (step - plain) % 2
+        targets += [out.at[0, :, pl.ds(j * width, width)] for j in range(count)]
+    for j in range(counts[3]):
+        targets += [outs[3].at[0, :, pl.ds(j * width, width)], outs[4].at[0, pl.ds(j * width, width)]]
+
+    def load(n):
+        return pltpu.make_async_copy(panels.at[n], inbox.at[n], in_sems.at[n])
+
+    def store(n):
+        return pltpu.make_async_copy(stage.at[n % SLOTS], targets[n], out_sems.at[n % SLOTS])
+
+    def put(n, value):
+        if n >= SLOTS:
+            store(n - SLOTS).wait()
+        stage[n % SLOTS] = value
+        store(n).start()
+
+    def widen(n):
+        load(n).wait()
+        put(n, inbox[n].astype(f32))
+
+    for n in range(plain):
+        load(n).start()
+    summed = (section == 0) if gathers else (section >= 0)
+    whole = [
+        pltpu.make_async_copy(src, dst, sems.at[n])
+        for n, (src, dst) in enumerate(((pool.at[1], rows), (pool.at[0], grads), (up_in, w_up), (down_in, w_down)))
+    ]
+
+    @pl.when(summed)
+    def _():
+        for n in range(plain, total):
+            load(n).start()
+
     if gathers:
-        width = rows.shape[1]
-        loads = [
-            pltpu.make_async_copy(src, dst, sems.at[n])
-            for n, (src, dst) in enumerate(
-                ((pool.at[1], rows), (pool.at[0], grads), (up_in, w_up), (down_in, w_down))
-            )
-        ]
-
-        @pl.when((step == 0) & (section == 1))
+
+        @pl.when(section == 1)
         def _():
-            for load in loads:
-                load.start()
-
-        @pl.when((step == plain) & (section == 1))
+            for copy in whole:
+                copy.start()
+
+    for n in range(plain):
+        widen(n)
+
+    @pl.when(summed)
+    def _():
+        for n in range(plain, total):
+            widen(n)
+
+    if gathers:
+
+        @pl.when(section == 1)
         def _():
-            for load in loads:
-                load.wait()
-
-        @pl.when((step >= plain) & (turn == 0) & (section == 1))
-        def _():
-            cols = at((step - plain) // 2 * width, width, width)
-            size = 512
-
-            @pl.loop(0, rows.shape[0] // size)
-            def _(i):
-                r = at(i * size, size, size)
-                e, s = gelu_both(nn(rows[r], w_up[:, cols]))
-                active[r] = e.astype(bf16)
-                bent[r] = (nt(grads[r], w_down[cols]) * s).astype(bf16)
-            up[0] = tn(rows[...], bent[...])
-
-        @pl.when((step >= plain) & (turn == 1) & (section == 1))
-        def _():
-            down[0] = tn(active[...], grads[...])
-
-    summed = (section == 0) if gathers else (section >= 0)
-
-    @pl.when((step >= plain) & (turn == 0) & summed)
-    def _():
-        up[0] = panels[0].astype(f32)
-
-    @pl.when((step >= plain) & (turn == 1) & summed)
-    def _():
-        down[0] = panels[0].astype(f32)
+            for copy in whole:
+                copy.wait()
+            size = rows.shape[0] // 4
+            for j in range(counts[3]):
+                cols = pl.ds(j * width, width)
+
+                @pl.loop(0, 4)
+                def _(i):
+                    r = at(i * size, size, size)
+                    e, s = gelu_both(nn(rows[r], w_up[:, cols]))
+                    active[r] = e.astype(bf16)
+                    bent[r] = (nt(grads[r], w_down[cols]) * s).astype(bf16)
+                put(plain + 2 * j, tn(rows[...], bent[...]))
+                put(plain + 2 * j + 1, tn(active[...], grads[...]))
+
+    for n in range(total - SLOTS, total):
+        store(n).wait()
 
 
 def finish(panels, pool, w_up, w_down, shapes, gathers):
     total, high, wide = panels.shape
     counts = [rows * columns // (high * wide) for rows, columns in shapes]
-    plain = sum(counts[:3])
-    out_specs = []
-    first = 0
-    for (rows, columns), count in zip(shapes[:3], counts):
-
-        def place_of(step, first=first, count=count):
-            return 0, 0, jnp.clip(step - first, 0, count - 1)
-
-        out_specs.append(pl.BlockSpec((1, high, wide), place_of))
-        first += count
-    out_specs.append(pl.BlockSpec((1, high, wide), lambda step: (0, 0, jnp.clip((step - plain) // 2, 0, counts[3] - 1))))
-    out_specs.append(pl.BlockSpec((1, high, wide), lambda step: (0, jnp.clip((step - plain - 1) // 2, 0, counts[4] - 1), 0)))
     there = pl.BlockSpec(memory_space=pl.ANY)
     gathered = pool.shape[1] if gathers else 16
     return pl.pallas_call(
         functools.partial(finish_kernel, counts, gathers),
-        grid=(total,),
         out_shape=[jax.ShapeDtypeStruct((1,) + shape, f32) for shape in shapes],
-        in_specs=[pl.BlockSpec((1, high, wide), lambda step: (step, 0, 0)), there, there, there],
-        out_specs=out_specs,
+        in_specs=[there] * 4,
+        out_specs=[there] * 5,
         scratch_shapes=[
+            pltpu.VMEM(panels.shape, bf16),
+            pltpu.VMEM((SLOTS, high, wide), f32),
             pltpu.VMEM((gathered, wide), bf16),
             pltpu.VMEM((gathered, wide), bf16),
             pltpu.VMEM(w_up.shape, bf16),
@@ -1010,8 +1011,10 @@
             pltpu.VMEM((gathered, wide), bf16),
             pltpu.VMEM((gathered, wide), bf16),
             pltpu.SemaphoreType.DMA((4,)),
+            pltpu.SemaphoreType.DMA((total,)),
+            pltpu.SemaphoreType.DMA((SLOTS,)),
         ],
-        compiler_params=pltpu.CompilerParams(vmem_limit_bytes=63 * 2**20),
+        compiler_params=pltpu.CompilerParams(vmem_limit_bytes=62 * 2**20),
     )(panels, pool, w_up, w_down)
 
 

time: 332 us -> 311 us (0.937)
  Pallas kernels: 311 us -> 290 us
    pallas_call x1, Pallas kernels: 159 us -> 143 us  [all_reduce(): pl.pallas_call(functools.partial(ar_kernel, [count * across_block // 2 fo...]
    pallas_call x1, Pallas kernels: 20.5 us -> 15.9 us  [finish(): pl.pallas_call(functools.partial(finish_kernel, counts, gathers), out_sha...]
where the time goes in v4:
time: 311 us; the launch traced here: 305 us
  Pallas kernels  290 us (93%)
  local copies, waits for them, and re-layouts  9.17 us (3%)
  other arithmetic  3.4 us (1%)
    pallas_call x1, Pallas kernels, all_reduce(): pl.pallas_call(functools.partial(ar_kernel, [count * across_block // 2 fo...  143 us
    pallas_call x1, Pallas kernels, fused(): pl.pallas_call(functools.partial(fused_kernel, items, span, dec_len, gath...  132 us
    pallas_call x1, Pallas kernels, finish(): pl.pallas_call(functools.partial(finish_kernel, counts, gathers), out_sha...  15.9 us

profile of v4, /device:TPU:0, one launch (start us, length us, event | category | flops | bytes accessed | tf_op | source)
XLA Modules:
  0.0 304.7 jit_solution(2060355600757492241)
XLA Ops:
  1.3 1.3 and_convert_fusion.1.key_open
  2.7 0.7 broadcast_in_dim.36
  3.4 0.1 broadcast_in_dim_reshape.3
  3.5 1.3 bitcast_convert_fusion
  4.8 0.7 and_convert_fusion.self_open
  5.5 1.5 copy.28
  7.1 1.2 pad.4.clone
  8.3 131.6 %shard_map.204 = (bf16[14,768,768]{2,1,0:T(8,128)(2,1)}, f32[8,768]{1,0:T(8,128)}, bf16[960,768]{1,0:T(8,128)(2,1)}, bf16[128,384]{1,0:T(8,128)(2,1)}, bf16[128,...) custom-call(bf16[960,768]{1,0:T(8,128)(2,1)} %bitcast.29, bf16[128,768]{1,0:T(8,128)(2,1)} %bitcast.34, ...), custom_call_target="tpu_custom_call" | custom-call | tf_op jit(solution)/shard_map/pallas_call | solution.py:579
  139.9 142.7 %shard_map.205 = (bf16[14,768,768]{2,1,0:T(8,128)(2,1)}, f32[8,768]{1,0:T(8,128)}, bf16[960,384]{1,0:T(8,128)(2,1)}) custom-call(bf16[14,768,768]{2,1,0:T(8,128)(2,1)} %get-tuple-element.25.g, f32[8,768]{1,0:T(8,128)} %get-tuple-element.26.norms, bf16[960,768]{1,0:T(8,128)(2,1)} %get-tuple-element.27.dx), custom_call_target="tpu_custom_call" | custom-call | tf_op jit(solution)/shard_map/pallas_call | solution.py:882
  282.6 1.2 slice.12
  283.8 1.1 copy.27
  284.9 0.8 slice_bitcast_fusion
  285.7 0.6 copy.26
  286.3 0.6 copy.25
  287.0 0.0 copy-start.1
  287.0 0.0 copy-start
  287.0 15.9 %shard_map.206 = (f32[1,768,2304]{2,1,0:T(8,128)}, f32[1,768,768]{2,1,0:T(8,128)}, f32[1,768,1536]{2,1,0:T(8,128)}, f32[1,768,3072]{2,1,0:T(8,128)}, f32[1,3072,768]{2,1,0:T(8,128)}) custom-call(bf16[14,768,768]{2,1,0:T(8,128)(2,1)} %get-tuple-element.30.panels, bf16[2,2048,768]{2,1,0:T(8,128)(2,1)} %bitcast.28, bf16[768,3072]{1,0:T(8,128)(2,1)} %bitcast.25, ...), custom_call_target="tpu_custom_call" | custom-call | tf_op jit(solution)/shard_map/pallas_call | solution.py:999
  302.9 0.0 copy-done.1
  302.9 0.6 copy.32
  303.5 0.0 copy-done
  303.5 0.6 copy.33
  (5 shorter events, 0.0 us)
Async XLA Ops:
  287.0 15.9 %copy-start.1 = (bf16[128,384]{1,0:T(8,128)(2,1)S(1)}, bf16[128,384]{1,0:T(8,128)(2,1)}, u32[]{:S(2)}) copy-start(bf16[128,384]{1,0:T(8,128)(2,1)} %get-tuple-element.24) | copy-start | bytes 294916
  287.0 16.6 %copy-start = (bf16[128,384]{1,0:T(8,128)(2,1)S(1)}, bf16[128,384]{1,0:T(8,128)(2,1)}, u32[]{:S(2)}) copy-start(bf16[128,384]{1,0:T(8,128)(2,1)} %get-tuple-element.29) | copy-start | bytes 294916
